TPU v7x, 512 devices: a whole 4x4x16 slice. The times are simulated.
512 devices in a mesh: dp: 32 (over y_lo, z), fsdp: 16 (over x, y_hi, core).
Axes of the slice: x: 4, y: 4 (y_hi: 2, y_lo: 2; y = y_hi * 2 + y_lo), z: 16, core: 2. Of those that a mesh axis runs over, the one named last changes fastest.
Arguments:
- train_layer_inputs: bfloat16 [320, 96, 8192], P('dp', None, 'fsdp'), may hold values from -6 to 6
- train_output_gradients: bfloat16 [320, 96, 8192], P('dp', None, 'fsdp'), may hold values from -6 to 6
- train_target_tokens: int32 [320, 96], P('dp'), may hold values from -100 to 128255, as said below
- validation_layer_inputs: bfloat16 [256, 96, 8192], P('dp', None, 'fsdp'), may hold values from -6 to 6
- validation_output_gradients: bfloat16 [256, 96, 8192], P('dp', None, 'fsdp'), may hold values from -6 to 6
- validation_target_tokens: int32 [256, 96], P('dp'), may hold values from -100 to 128255, as said below
- adapter_down: bfloat16 [64, 8192], P(None, 'fsdp'), may hold values from -0.0625 to 0.0625
- adapter_up: bfloat16 [64, 8192], P(None, 'fsdp'), may hold values from -0.0625 to 0.0625
- adam_first_moments: float32 [2, 64, 8192], P(None, None, 'fsdp'), may hold values from -0.4375 to 0.4375
- adam_second_moments: float32 [2, 64, 8192], P(None, None, 'fsdp'), may hold values from 0.0001 to 0.01
- rank_projection: bfloat16 [2, 64, 16], replicated, may hold values from -0.75 to 0.75
- feature_projection: bfloat16 [2, 8192, 256], P(None, 'fsdp')
Outputs:
- cosine: float32 [320, 256], P('dp', 'fsdp')
Inputs may be any that keep to these rules, and one draw needn't show every extreme that they name: `train_target_tokens`: each segment begins with one or more positions labelled -100; at least its last 24 positions hold token ids below 128256. `validation_target_tokens`: each segment begins with one or more positions labelled -100; at least its last 24 positions hold token ids below 128256.
All inputs are finite; a program needn't handle non-finite values.
Results may differ from a plain program's by a relative error of at most 0.0055.
Values sent between devices are 32-bit elements; how exact they have to be, the bound alone decides.
A program may use at most 64 MiB of HBM per device.

v0:
```python
import jax
import jax.numpy as jnp
from jax import lax
from jax.sharding import PartitionSpec as P

ADAPTER_SCALE = 2.0
BETA_FIRST = 0.9
BETA_SECOND = 0.999
ADAM_EPS = 1e-08
NORM_EPS = 1e-06


def inner_products(layer_inputs, output_gradient, adapter_down, adapter_up):
    down_inner_product = jnp.einsum(
        "tgc,qc->tgq", layer_inputs, adapter_down, preferred_element_type=jnp.float32
    )
    up_inner_product = jnp.einsum(
        "tgc,qc->tgq", output_gradient, adapter_up, preferred_element_type=jnp.float32
    )
    return jnp.concatenate([down_inner_product, up_inner_product], axis=2)


def segment_gradient(layer_inputs, output_gradient, labels, summed, adapted_output):
    rank_count = summed.shape[2] // 2
    retained_mask = (labels != -100).astype(jnp.float32)
    if adapted_output:
        weight_values = retained_mask * (
            ADAPTER_SCALE / jnp.sum(retained_mask, axis=1, keepdims=True)
        )
    else:
        weight_values = retained_mask
    scaled = (summed * weight_values[:, :, None]).astype(jnp.bfloat16)
    grad_down = jnp.einsum(
        "esr,esd->erd", scaled[:, :, rank_count:], layer_inputs, preferred_element_type=jnp.float32
    )
    grad_up = jnp.einsum(
        "esr,esd->erd",
        scaled[:, :, :rank_count],
        output_gradient,
        preferred_element_type=jnp.float32,
    )
    return jnp.stack([grad_down, grad_up], axis=1)


def body(
    train_layer_inputs,
    train_output_gradients,
    train_target_tokens,
    validation_layer_inputs,
    validation_output_gradients,
    validation_target_tokens,
    adapter_down,
    adapter_up,
    adam_first_moments,
    adam_second_moments,
    rank_projection,
    feature_projection,
):
    train_input_pair = inner_products(
        train_layer_inputs, train_output_gradients, adapter_down, adapter_up
    )
    validation_input_pair = inner_products(
        validation_layer_inputs, validation_output_gradients, adapter_down, adapter_up
    )
    train_input_pair, validation_input_pair = lax.psum(
        (train_input_pair, validation_input_pair), "fsdp"
    )
    train_grad = segment_gradient(
        train_layer_inputs, train_output_gradients, train_target_tokens, train_input_pair, True
    )
    valid_grad = segment_gradient(
        validation_layer_inputs,
        validation_output_gradients,
        validation_target_tokens,
        validation_input_pair,
        False,
    )
    first_moment = BETA_FIRST * adam_first_moments + (1.0 - BETA_FIRST) * train_grad
    second_moment = (
        BETA_SECOND * adam_second_moments + (1.0 - BETA_SECOND) * train_grad * train_grad
    )
    train_dir = (first_moment / (jnp.sqrt(second_moment) + ADAM_EPS)).astype(jnp.bfloat16)
    valid_dir = valid_grad.astype(jnp.bfloat16)
    left_wide = rank_projection.astype(jnp.float32)
    train_rows = jnp.einsum(
        "ecrd,cdk->ecrk", train_dir, feature_projection, preferred_element_type=jnp.float32
    )
    valid_rows = jnp.einsum(
        "ecrd,cdk->ecrk", valid_dir, feature_projection, preferred_element_type=jnp.float32
    )
    train_rows, valid_rows = (
        lax.psum_scatter(train_rows, "fsdp", scatter_dimension=3, tiled=True),
        lax.psum_scatter(valid_rows, "fsdp", scatter_dimension=3, tiled=True),
    )
    train_feat = jnp.einsum(
        "cra,ecrk->ecak", left_wide, train_rows, precision=lax.Precision.HIGHEST
    )
    valid_feat = jnp.einsum(
        "cra,ecrk->ecak", left_wide, valid_rows, precision=lax.Precision.HIGHEST
    )
    train_norm, valid_norm = lax.psum(
        (
            jnp.sum(train_feat * train_feat, axis=(1, 2, 3)),
            jnp.sum(valid_feat * valid_feat, axis=(1, 2, 3)),
        ),
        "fsdp",
    )
    train_unit = train_feat / jnp.sqrt(train_norm + NORM_EPS)[:, None, None, None]
    valid_unit = valid_feat / jnp.sqrt(valid_norm + NORM_EPS)[:, None, None, None]
    partial_cos = jnp.einsum(
        "eabk,vabk->ev",
        train_unit,
        lax.all_gather(valid_unit, "dp", axis=0, tiled=True),
        precision=lax.Precision.HIGHEST,
    )
    return lax.psum_scatter(partial_cos, "fsdp", scatter_dimension=1, tiled=True)


def solution(mesh):
    placed = (
        P("dp", None, "fsdp"),
        P("dp", None, "fsdp"),
        P("dp", None),
        P("dp", None, "fsdp"),
        P("dp", None, "fsdp"),
        P("dp", None),
        P(None, "fsdp"),
        P(None, "fsdp"),
        P(None, None, "fsdp"),
        P(None, None, "fsdp"),
        P(),
        P(None, "fsdp", None),
    )
    return jax.shard_map(
        body, mesh=mesh, in_specs=placed, out_specs=P("dp", "fsdp"), check_vma=False
    )
```

profile of v0, /device:TPU:1, one launch (start us, length us, event | category | flops | bytes accessed | tf_op | source)
XLA Modules:
  0.0 601.2 jit_solution(16834612925558382231)
XLA Ops:
  6.5 0.0 copy-start
  6.5 0.0 all-reduce.4.cloned.1.call-start
  6.5 1.7 fusion.25
  8.2 1.7 fusion.27
  9.9 0.0 copy-done.2
  9.9 1.2 fusion.21
  11.1 0.0 copy-done
  11.2 0.0 copy-done.7
  11.2 0.0 copy-start.9
  11.2 0.0 copy-start.10
  11.2 0.5 fusion.23
  11.7 0.9 pad_maximum_fusion.2
  12.5 0.9 pad_maximum_fusion.1
  13.4 0.0 all-reduce.4.cloned.1.call-update
  13.5 0.0 reduce-scatter.8.cloned.1.call-start
  13.5 0.1 convert_reduce_fusion
  13.7 161.7 %all-reduce.4.cloned.1.call-done = (f32[10,96,128]{1,2,0:T(8,128)}, f32[8,96,128]{1,2,0:T(8,128)}) async-done(((f32[10,96,128]{1,2,0:T(8,128)}, f32[8,96,128]{1,2,0:T(8,128)}), (f32[10,96,128]{1,2,0:T(8,128)}, f32[8,96,128]{1,2,0:T(8,128)})) %all-reduce.4.cloned.1.call-update) | async-done | bytes 884752 | tf_op jit(solution)/shard_map/psum | solution.py:65
  175.4 1.1 multiply_convert_fusion.1
  176.5 0.3 fusion.11
  176.8 0.3 fusion.10
  177.1 0.0 copy-start.6
  177.1 2.1 convolution_bitcast_fusion.1
  179.2 0.0 reduce-scatter.8.cloned.1.call-update
  179.2 0.0 copy-start.1
  179.2 0.0 reduce-scatter.6.cloned.1.call-start
  179.3 0.1 broadcast_select_fusion
  179.4 1.1 broadcast_multiply_fusion
  180.5 0.0 copy-done.4
  180.5 0.1 multiply_convert_fusion
  180.5 0.3 convolution_bitcast_fusion.2
  180.9 0.3 convolution_bitcast_fusion.3
  181.2 3.3 convolution_bitcast_fusion
  184.5 0.0 reduce-scatter.6.cloned.1.call-update
  184.6 0.0 reduce-scatter.10.cloned.1.call-start
  184.6 89.1 %reduce-scatter.8.cloned.1.call-done = f32[8,2,64,16]{2,3,0,1:T(8,128)} async-done(((f32[8,2,64,256]{2,3,0,1:T(8,128)}), f32[8,2,64,16]{2,3,0,1:T(8,128)}) %reduce-scatter.8.cloned.1.call-update) | async-done | bytes 65552 | tf_op jit(solution)/shard_map/reduce_scatter | solution.py:93
  273.7 1.2 multiply_reduce_fusion.1
  274.9 99.8 %reduce-scatter.6.cloned.1.call-done = f32[10,2,64,16]{2,3,0,1:T(8,128)} async-done(((f32[10,2,64,256]{2,3,0,1:T(8,128)}), f32[10,2,64,16]{2,3,0,1:T(8,128)}) %reduce-scatter.6.cloned.1.call-update) | async-done | bytes 81936 | tf_op jit(solution)/shard_map/reduce_scatter | solution.py:92
  374.8 1.3 multiply_reduce_fusion
  376.0 34.3 %all-reduce = (f32[10]{0:T(128)S(1)}, f32[8]{0:T(128)S(1)}) all-reduce(f32[10]{0:T(128)S(1)} %get-tuple-element.11, f32[8]{0:T(128)S(1)} %get-tuple-element.13), channel_id=1, replica_groups=mesh['dp'=32,'fsdp'=16] {'fsdp'}, use_global_device_ids=true, to_apply=%region_4.0 | all-reduce | flops 18 | bytes 144 | tf_op jit(solution)/shard_map/psum | solution.py:101
  410.4 0.1 divide_bitcast_fusion
  410.5 0.2 copy.15
  410.7 0.1 divide_bitcast_fusion.1
  410.8 83.4 %all_gather.3 = f32[256,2,16,16]{2,3,0,1:T(8,128)} all-gather(f32[8,2,16,16]{2,3,0,1:T(8,128)S(1)} %divide_bitcast_fusion.1), channel_id=1, replica_groups=mesh['dp'=32,'fsdp'=16] {'dp'}, dimensions={0}, use_global_device_ids=true | all-gather | bytes 540672 | tf_op jit(solution)/shard_map/all_gather | solution.py:113
  494.2 5.7 copy.16
  499.8 5.8 convolution_bitcast_fusion.4
  505.6 0.0 reduce-scatter.10.cloned.1.call-update
  505.7 87.6 %reduce-scatter.10.cloned.1.call-done = f32[16,10]{1,0:T(8,128)} async-done(((f32[256,10]{1,0:T(8,128)}), f32[16,10]{1,0:T(8,128)}) %reduce-scatter.10.cloned.1.call-update) | async-done | bytes 656
  593.3 1.4 copy.21
  (17 shorter events, 0.1 us)
Async XLA Ops:
  6.5 4.6 copy-start
  6.5 4.6 copy-start.7
  6.5 3.4 copy-start.2
  6.5 168.9 %all-reduce.4.cloned.1.call-start = ((), (), s32[]{:S(2)}) async-start(), calls=%async_computation.6 | async-start | bytes 2359296 | tf_op jit(solution)/shard_map/psum | solution.py:65
  11.2 2.3 copy-start.9
  11.2 2.5 copy-start.10
  12.5 164.3 %copy-start.3 = (bf16[8,96,512]{2,1,0:T(8,128)(2,1)S(1)}, bf16[8,96,512]{2,1,0:T(8,128)(2,1)}, u32[]{:S(2)}) copy-start(bf16[8,96,512]{2,1,0:T(8,128)(2,1)} %param.15) | copy-start | bytes 2359300
  13.4 163.7 %copy-start.5 = (bf16[2,512,256]{2,1,0:T(8,128)(2,1)S(1)}, bf16[2,512,256]{2,1,0:T(8,128)(2,1)}, u32[]{:S(2)}) copy-start(bf16[2,512,256]{2,1,0:T(8,128)(2,1)} %param.23) | copy-start | bytes 1572868
  13.5 260.3 %reduce-scatter.8.cloned.1.call-start = ((), (), s32[]{:S(2)}) async-start(), calls=%async_computation.4 | async-start | bytes 2228224 | tf_op jit(solution)/shard_map/reduce_scatter | solution.py:93
  177.1 2.3 copy-start.6
  177.1 3.4 copy-start.4
  179.2 1.6 copy-start.1
  179.2 195.5 %reduce-scatter.6.cloned.1.call-start = ((), (), s32[]{:S(2)}) async-start(), calls=%async_computation.3 | async-start | bytes 2785280 | tf_op jit(solution)/shard_map/reduce_scatter | solution.py:92
  184.5 89.2 %copy-start.8 = (bf16[2,64,16]{1,2,0:T(8,128)(2,1)S(1)}, bf16[2,64,16]{1,2,0:T(8,128)(2,1)}, u32[]{:S(2)}) copy-start(bf16[2,64,16]{1,2,0:T(8,128)(2,1)} %param.22) | copy-start | bytes 12292
  184.6 408.7 %reduce-scatter.10.cloned.1.call-start = ((), (), s32[]{:S(2)}) async-start(), calls=%async_computation.5 | async-start | bytes 139264
Sparse Core Ops, SparseCore 0:
  13.6 161.7 all-reduce.3
  180.2 93.4 reduce-scatter.7
  278.6 96.1 reduce-scatter.5
  505.8 87.4 reduce-scatter.9
where the time goes:
time: 602 us; the launch traced here: 601 us
  waiting for transfers between devices  438 us (73%)
  blocking collectives  118 us (20%)
  matrix products  20 us (3%)
  between operations  13.3 us (2%)
  local copies, waits for them, and re-layouts  7.24 us (1%)
    psum x1, waiting for transfers between devices, body(): lax.psum((train_input_pair, validation_input_pair), 'fsdp')  162 us
    reduce_scatter x1, waiting for transfers between devices, body(): lax.psum_scatter(train_rows, 'fsdp', scatter_dimension=3, tiled=True)  99.8 us
    reduce_scatter x1, waiting for transfers between devices, body(): lax.psum_scatter(valid_rows, 'fsdp', scatter_dimension=3, tiled=True)  89.1 us
    unnamed x5, waiting for transfers between devices  87.7 us
    all_gather x1, blocking collectives, body(): lax.all_gather(valid_unit, 'dp', axis=0, tiled=True)  83.4 us
    psum x1, blocking collectives, body(): lax.psum((jnp.sum(train_feat * train_feat, axis=(1, 2, 3)), jnp.sum(valid...  34.3 us
  transfers between devices with their start and end apart: 4, of which 4 were waited for; matrix products, arithmetic and copies ran while one was open for 1% of the time, Pallas kernels for 0%

commit v1 on v0

v1 whole, which is shorter than its diff:
```python
import jax
import jax.numpy as jnp
from jax import lax
from jax.experimental import pallas as pl
from jax.experimental.pallas import tpu as pltpu
from jax.sharding import PartitionSpec as P

ADAPTER_SCALE = 2.0
BETA_FIRST = 0.9
BETA_SECOND = 0.999
ADAM_EPS = 1e-08
NORM_EPS = 1e-06

MESH = pl.DeviceIdType.MESH
F32 = jnp.float32
BF16 = jnp.bfloat16
SEG = 96
NT = 960
NV = 768
HALF = 512

OFFSETS = ((2, 1), (1, 1), (3, 1), (2, 0), (0, 1), (1, 0), (3, 0))
PAIR_OFFSETS = (4, 3, 5, 2, 6, 1, 7, 0)


def dot(a, b):
    return lax.dot_general(a, b, (((1,), (0,)), ((), ())), preferred_element_type=F32)


def dot_nt(a, b, precision=None):
    return lax.dot_general(
        a, b, (((1,), (1,)), ((), ())), preferred_element_type=F32, precision=precision
    )


def split(x):
    hi = x.astype(BF16)
    return hi, (x - hi.astype(F32)).astype(BF16)


def kernel(
    xt, ct, lt, xv, cv, lv, ad, au, mom1, mom2, rank_p, feat_p,
    out,
    buf, w, rp, fp, m_, v_, labt, labv,
    zp, ztw, ar, zf, wt, bd, pm8, pm2, dirs,
    pvl, pvtw, bvr, ptl, pttw, btr, vs, ts, vg, tg, ds, dr,
    ld, s_tw, r_tw, s_a1, r_a1, s_a2, r_a2, s_fw, r_fw, s_bv, r_bv, s_bt, r_bt,
    s_c, r_c, s_q, r_q, s_d, r_d, tok,
):
    d = lax.axis_index("dp")
    f = lax.axis_index("fsdp")
    y, z = lax.div(d, 16), lax.rem(d, 16)
    zm, zr = lax.div(z, 2), lax.rem(z, 2)
    q, k = lax.div(f, 2), lax.rem(f, 2)
    x, yh = lax.div(q, 2), lax.rem(q, 2)
    other = 1 - k
    twin = (d, f + 1 - 2 * k)
    chips = []
    for dx, dy in OFFSETS:
        to = lax.rem(x + dx, 4) * 2 + lax.rem(yh + dy, 2)
        fro = lax.rem(x + 4 - dx, 4) * 2 + lax.rem(yh + dy, 2)
        chips.append((to, fro))

    def dp_at(y_at, z_at):
        return y_at * 16 + z_at

    def z_off(n):
        return dp_at(y, lax.rem(z + n + 16, 16))

    loads = [
        (au, w.at[0]),
        (ad, w.at[1]),
        (rank_p, rp),
        (ct, buf.at[0, pl.ds(0, NT)]),
        (cv, buf.at[0, pl.ds(NT, NV)]),
        (xt, buf.at[1, pl.ds(0, NT)]),
        (xv, buf.at[1, pl.ds(NT, NV)]),
        (lt, labt),
        (lv, labv),
        (feat_p, fp),
        (mom1, m_),
        (mom2, v_),
    ]
    load = [pltpu.make_async_copy(a, b, ld.at[i]) for i, (a, b) in enumerate(loads)]
    for cp in load:
        cp.start()

    barrier = pltpu.get_barrier_semaphore()
    zt = z + 1 - 2 * zr
    greet = [(d, to * 2 + k) for to, _ in chips]
    greet += [twin, (dp_at(1 - y, z), f), (dp_at(y, zt), f), (dp_at(1 - y, zt), f)]
    greet += [(dp_at(y, lax.rem(z + 15 + 2 * zr, 16)), f)]
    for peer in greet:
        pl.semaphore_signal(barrier, inc=1, device_id=peer, device_id_type=MESH)

    def remote(src, dst, send, recv, peer):
        return pltpu.make_async_remote_copy(
            src_ref=src, dst_ref=dst, send_sem=send, recv_sem=recv,
            device_id=peer, device_id_type=MESH,
        )

    lane = lax.broadcasted_iota(jnp.int32, (16, 128), 1)

    def inner(c, at):
        wc = w[c]
        proj = lax.dot_general(
            rp[c], wc, (((0,), (0,)), ((), ())), preferred_element_type=F32
        )
        hi, lo = split(proj)
        both = jnp.concatenate([hi, lo], axis=0)
        for t in range(4):
            o = dot_nt(wc, buf[c, pl.ds(256 * t, 256), :])
            zp[at, :, 2 * t] = o[:, :128].reshape(8, 8, 128)
            if t < 3:
                zp[at, :, 2 * t + 1] = o[:, 128:].reshape(8, 8, 128)
            else:
                tail = o[:, 128:]
        for g in range(4):
            rows = jnp.concatenate(
                [
                    buf[c, pl.ds(NT + 192 * g, 128), :],
                    buf[c, pl.ds(NT + 192 * g + 64, 128), :],
                ],
                axis=0,
            )
            o = dot_nt(both, rows)
            o = o[:16] + o[16:]
            zp[at, 2 * g : 2 * g + 2, 8] = o[:, :128].reshape(2, 8, 128)
            mixed = jnp.where(lane < 64, tail[16 * g : 16 * g + 16], o[:, 128:])
            zp[at, 2 * g : 2 * g + 2, 7] = mixed.reshape(2, 8, 128)

    for i in range(7):
        load[i].wait()
    inner(other, 0)
    pl.semaphore_wait(barrier, len(greet))
    tw_a = remote(zp.at[0], ztw, s_tw.at[0], r_tw.at[0], twin)
    tw_a.start()
    for n in (-1, 1):
        pl.semaphore_signal(tok.at[0], inc=1, device_id=(z_off(n), f), device_id_type=MESH)
    inner(k, 1)
    tw_a.wait_recv()
    zp[1] = zp[1] + ztw[...]
    a1 = [
        remote(zp.at[1, to], ar.at[i], s_a1.at[i], r_a1.at[i], (d, to * 2 + k))
        for i, (to, _) in enumerate(chips)
    ]
    for cp in a1:
        cp.start()

    for i in range(7, 12):
        load[i].wait()
    iota = lambda shape, dim: lax.broadcasted_iota(jnp.int32, shape, dim)
    one = lambda cond: jnp.where(cond, 1.0, 0.0)
    tl = iota((1, 1024), 1)
    seg = jnp.zeros((1, 1024), jnp.int32)
    for j in range(1, 11):
        seg = seg + jnp.where(tl >= SEG * j, 1, 0)
    kept = one(labt[...] != -100)
    scale = ADAPTER_SCALE / jnp.sum(kept, axis=1, keepdims=True)
    spread = one(iota((SEG, 1024), 0) == tl - SEG * seg).astype(BF16)
    laid = dot(kept.astype(BF16), spread)
    wt[0:10, :] = jnp.where(iota((10, 1024), 0) == seg, laid * scale, 0.0)
    grp = lax.shift_right_logical(tl, 8)
    u = tl - 256 * grp
    tokv = jnp.where(u < 128, u, u - 64)
    valid = jnp.where(u < 128, 1, jnp.where(u >= 192, 1, 0))
    late = jnp.where(tokv >= SEG, 1, 0)
    segv = jnp.where(valid > 0, 2 * grp + late, -1)
    keptv = one(labv[...] != -100)
    spread = one(iota((SEG, 1024), 0) == tokv - SEG * late).astype(BF16)
    bd[...] = jnp.where(iota((8, 1024), 0) == segv, dot(keptv.astype(BF16), spread), 0.0)
    up8 = one(lax.shift_right_logical(iota((128, 16), 0), 3) == iota((128, 16), 1)).astype(BF16)
    up2 = one(lax.shift_right_logical(iota((32, 16), 0), 1) == iota((32, 16), 1)).astype(BF16)
    wide = one((iota((64, HALF), 1) & 63) == iota((64, HALF), 0)).astype(BF16)
    in8 = (iota((128, HALF), 0) & 7) == lax.shift_right_logical(iota((128, HALF), 1), 6)
    in2 = (iota((32, 128), 0) & 1) == lax.shift_right_logical(iota((32, 128), 1), 6)
    for c in range(2):
        pc = rp[c]
        a8 = dot(dot_nt(up8, pc).astype(BF16), wide)
        pm8[c] = jnp.where(in8, a8, 0.0).astype(BF16)
        a2 = dot(dot_nt(up2, pc).astype(BF16), wide[:, :128])
        pm2[c] = jnp.where(in2, a2, 0.0).astype(BF16)

    pl.semaphore_wait(tok.at[0], 2)
    for n in (-2, 2):
        pl.semaphore_signal(tok.at[1], inc=1, device_id=(z_off(n), f), device_id_type=MESH)

    total = zp[1, q]
    for i in reversed(range(7)):
        a1[i].wait_recv()
        total = total + ar[i]
    zf[k, q] = total
    a2 = [
        remote(zf.at[k, q], zf.at[k, q], s_a2.at[i], r_a2.at[i], (d, to * 2 + k))
        for i, (to, _) in enumerate(chips)
    ]
    for cp in a2:
        cp.start()
    fw = [None] * 8
    fw[7] = remote(zf.at[k, q], zf.at[k, q], s_fw.at[7], r_fw.at[7], twin)
    fw[7].start()
    pl.semaphore_wait(tok.at[1], 2)
    for n in (-4, 4):
        pl.semaphore_signal(tok.at[2], inc=1, device_id=(z_off(n), f), device_id_type=MESH)
    for i in reversed(range(7)):
        fro = chips[i][1]
        remote(zf.at[k, fro], zf.at[k, fro], s_a2.at[i], r_a2.at[i], twin).wait_recv()
        fw[i] = remote(zf.at[k, fro], zf.at[k, fro], s_fw.at[i], r_fw.at[i], twin)
        fw[i].start()

    def valid_features(c, at):
        lhs, rhs = [], []
        for g in range(4):
            za = zf[c, 2 * g : 2 * g + 2, 8].reshape(16, 128)
            zb = zf[c, 2 * g : 2 * g + 2, 7].reshape(16, 128)
            zg = jnp.concatenate([za, zb], axis=1)
            hi = zg.astype(BF16).astype(F32)
            lo = zg - hi
            mask = bd[:, 256 * g : 256 * g + 256]
            blocks = [
                jnp.broadcast_to(part[a : a + 1], (8, 256)) * mask
                for part in (hi, lo)
                for a in range(16)
            ]
            lhs.append(jnp.concatenate(blocks, axis=0).astype(BF16))
        left = []
        for n in range(2):
            cols = pl.ds(256 * n, 256)
            acc = None
            for g in range(4):
                rows = jnp.concatenate(
                    [
                        buf[1 - c, pl.ds(NT + 192 * g, 128), cols],
                        buf[1 - c, pl.ds(NT + 192 * g + 64, 128), cols],
                    ],
                    axis=0,
                )
                o = dot(lhs[g], rows)
                acc = o if acc is None else acc + o
            left.append(acc[:128] + acc[128:])
        hi, lo = split(jnp.concatenate(left, axis=1))
        o = dot(jnp.concatenate([hi, lo], axis=0), fp[c])
        o = o[:128] + o[128:]
        for h in range(2):
            part = o[:, 128 * h : 128 * h + 128].reshape(8, 2, 8, 128)
            for a2_ in range(2):
                pvl[at, :, 2 * a2_ + h] = part[:, a2_]

    def train_pair(c, i):
        t0 = (192 * i) // 128
        zg = jnp.concatenate(
            [zf[c, :, t0].reshape(64, 128), zf[c, :, t0 + 1].reshape(64, 128)], axis=1
        )
        cols = pl.ds(128 * t0, 256)
        lhs = jnp.concatenate(
            [zg * wt[2 * i : 2 * i + 1, cols], zg * wt[2 * i + 1 : 2 * i + 2, cols]], axis=0
        ).astype(BF16)
        for n in range(2):
            at = pl.ds(256 * n, 256)
            g2 = dot(lhs, buf[1 - c, pl.ds(128 * t0, 256), at])
            m = BETA_FIRST * m_[c, :, at]
            v = BETA_SECOND * v_[c, :, at]
            for s in range(2):
                g = g2[64 * s : 64 * s + 64]
                num = m + (1.0 - BETA_FIRST) * g
                second = v + (1.0 - BETA_SECOND) * g * g
                den = second * lax.rsqrt(second) + ADAM_EPS
                dirs[pl.ds(128 * i + 64 * s, 64), at] = (num / den).astype(BF16)

    def train_features(c, at):
        l8 = dot(pm8[c], dirs[pl.ds(0, 512), :])
        l2 = dot(pm2[c], dirs[pl.ds(512, 128), :])
        hi, lo = split(jnp.concatenate([l8, l2], axis=0))
        o = dot(jnp.concatenate([hi, lo], axis=0), fp[c])
        o = o[:160] + o[160:]
        for h in range(2):
            cols = o[:, 128 * h : 128 * h + 128]
            part = cols[:128].reshape(8, 2, 8, 128)
            for a2_ in range(2):
                ptl[at, :, 2 * a2_ + h] = part[:, a2_]
            for p in range(8):
                ptl[at, p, 4, pl.ds(4 * h, 4), :] = cols[128 + 4 * p : 132 + 4 * p]

    valid_features(k, 1)
    for i in range(8):
        at = q if i == 7 else chips[i][1]
        remote(
            zf.at[other, at], zf.at[other, at], s_fw.at[i], r_fw.at[i], twin
        ).wait_recv()
    valid_features(other, 0)
    tw_v = remote(pvl.at[0], pvtw, s_tw.at[1], r_tw.at[1], twin)
    tw_v.start()
    for i in range(5):
        train_pair(other, i)
        if i == 1:
            tw_v.wait_recv()
            pvl[1] = pvl[1] + pvtw[...]
            b_v = [
                remote(pvl.at[1, to], bvr.at[j], s_bv.at[j], r_bv.at[j], (d, to * 2 + k))
                for j, (to, _) in enumerate(chips)
            ]
            for cp in b_v:
                cp.start()
    train_features(other, 0)
    tw_t = remote(ptl.at[0], pttw, s_tw.at[2], r_tw.at[2], twin)
    tw_t.start()

    par = lax.rem(zm, 2)
    slot = lax.div(zm, 2) * 2 + zr
    mine = zr == par
    c_v = []
    for j in PAIR_OFFSETS:
        peer = (dp_at(y, 2 * lax.rem(zm + j, 8) + par), f)
        c_v.append(remote(vs, vg.at[slot], s_c.at[j], r_c.at[slot], peer))
    keep_v = pltpu.make_async_copy(vs, vg.at[slot], r_c.at[slot])

    for i in range(5):
        train_pair(k, i)
        if i == 2:
            pl.semaphore_wait(tok.at[2], 2)
            total = pvl[1, q]
            for j in reversed(range(7)):
                b_v[j].wait_recv()
                total = total + bvr[j]
            vs[...] = total
            for cp in c_v[:7]:
                cp.start()

            @pl.when(mine)
            def _():
                keep_v.start()

            @pl.when(jnp.logical_not(mine))
            def _():
                c_v[7].start()

    train_features(k, 1)
    tw_t.wait_recv()
    ptl[1] = ptl[1] + pttw[...]
    b_t = [
        remote(ptl.at[1, to], btr.at[j], s_bt.at[j], r_bt.at[j], (d, to * 2 + k))
        for j, (to, _) in enumerate(chips)
    ]
    for cp in b_t:
        cp.start()
    total = ptl[1, q]
    for j in reversed(range(7)):
        b_t[j].wait_recv()
        total = total + btr[j]
    ts[...] = total
    blk = 2 * y + zr
    tg[blk] = total
    partners = (
        (1 - y, zt, 2 * (1 - y) + 1 - zr),
        (1 - y, z, 2 * (1 - y) + zr),
        (y, zt, 2 * y + 1 - zr),
    )
    q_t = [
        remote(ts, tg.at[blk], s_q.at[j], r_q.at[j], (dp_at(py, pz), f))
        for j, (py, pz, _) in enumerate(partners)
    ]
    for cp in q_t:
        cp.start()
    for i in range(8):
        pltpu.make_async_copy(vs, vg.at[i], r_c.at[i]).wait()
    vals = jnp.concatenate([vg[:, t].reshape(64, 128) for t in range(4)], axis=1)
    ones = jnp.ones((8, HALF), F32)
    nv = dot_nt(ones, vals * vals, lax.Precision.HIGHEST)
    for j, (_, _, pb) in enumerate(partners):
        remote(ts, tg.at[pb], s_q.at[j], r_q.at[j], twin).wait_recv()

    tail = tg[:, 4].reshape(32, 128)
    row = iota((32, 128), 0) & 7
    quarter = 2 * (lax.shift_right_logical(row, 1) & 1) + lax.shift_right_logical(row, 2)
    lhs = []
    na = jnp.zeros((32, 1), F32)
    for t in range(4):
        top = tg[:, t].reshape(32, 128)
        na = na + jnp.sum(top * top, axis=1, keepdims=True)
        lhs.append(jnp.concatenate([top, jnp.where(quarter == t, tail, 0.0)], axis=0))
    nb = jnp.sum(tail * tail, axis=1, keepdims=True)
    cos = dot_nt(jnp.concatenate(lhs, axis=1), vals, lax.Precision.HIGHEST)
    nv4 = jnp.concatenate([nv] * 4, axis=0)
    half32 = lambda n: jnp.broadcast_to(n, (32, 32))
    msg_a = jnp.concatenate([cos[:32], nv4], axis=1)
    msg_b = jnp.concatenate([cos[32:], half32(na), half32(nb)], axis=1)
    ds[:, 0] = msg_a.reshape(4, 8, 128)
    ds[:, 1] = msg_b.reshape(4, 8, 128)
    d_c = []
    for by in range(2):
        for br in range(2):
            for i in range(4):
                to_f = 8 * y + 2 * i + zr
                b = 2 * by + br
                j = 4 * b + i
                here = jnp.logical_and(jnp.logical_and(y == by, zr == br), f == to_f)
                cp = remote(
                    ds.at[b], dr.at[f], s_d.at[j], r_d.at[f], (dp_at(by, 2 * zm + br), to_f)
                )
                keep = pltpu.make_async_copy(ds.at[b], dr.at[f], r_d.at[f])
                d_c.append((cp, here))

                @pl.when(jnp.logical_not(here))
                def _():
                    cp.start()

                @pl.when(here)
                def _():
                    keep.start()

    for cp in [tw_a, tw_v, tw_t] + a1 + a2 + fw + b_v + b_t + c_v[:7] + q_t:
        cp.wait_send()

    @pl.when(jnp.logical_not(mine))
    def _():
        c_v[7].wait_send()

    for i in range(16):
        pltpu.make_async_copy(ds.at[0], dr.at[i], r_d.at[i]).wait()
    sa = dr[0, 0]
    sb = dr[0, 1]
    for i in range(1, 16):
        sa = sa + dr[i, 0]
        sb = sb + dr[i, 1]
    inv_v = lax.rsqrt(sa[:, 64:128] + NORM_EPS)
    res_a = sa[:, 0:64] * lax.rsqrt(sb[:, 64:65] + NORM_EPS) * inv_v
    s2 = (sb[0:2] + sb[2:4]) + (sb[4:6] + sb[6:8])
    res_b = s2[:, 0:64] * lax.rsqrt(s2[:, 96:97] + NORM_EPS) * inv_v[0:2]
    pick = lax.rem(lax.div(f, 2), 4)
    for res, rows in ((res_a, pl.ds(0, 8)), (res_b, pl.ds(8, 2))):
        o = res[:, 0:16]
        for i in range(1, 4):
            o = jnp.where(pick == i, res[:, 16 * i : 16 * i + 16], o)
        out[rows, :] = o
    for cp, here in d_c:

        @pl.when(jnp.logical_not(here))
        def _():
            cp.wait_send()


def body(xt, ct, lt, xv, cv, lv, ad, au, mom1, mom2, rank_p, feat_p):
    dma = pltpu.SemaphoreType.DMA
    tile = lambda *lead: pltpu.VMEM(lead + (8, 128), F32)
    scratch = [
        pltpu.VMEM((2, NT + NV, HALF), BF16),
        pltpu.VMEM((2, 64, HALF), BF16),
        pltpu.VMEM((2, 64, 16), BF16),
        pltpu.VMEM((2, HALF, 256), BF16),
        pltpu.VMEM((2, 64, HALF), F32),
        pltpu.VMEM((2, 64, HALF), F32),
        pltpu.VMEM((10, SEG), jnp.int32),
        pltpu.VMEM((8, SEG), jnp.int32),
        tile(2, 8, 9),
        tile(8, 9),
        tile(7, 9),
        tile(2, 8, 9),
        pltpu.VMEM((16, 1024), F32),
        pltpu.VMEM((8, 1024), F32),
        pltpu.VMEM((2, 128, HALF), BF16),
        pltpu.VMEM((2, 32, 128), BF16),
        pltpu.VMEM((640, HALF), BF16),
        tile(2, 8, 4),
        tile(8, 4),
        tile(7, 4),
        tile(2, 8, 5),
        tile(8, 5),
        tile(7, 5),
        tile(4),
        tile(5),
        tile(8, 4),
        tile(4, 5),
        tile(4, 2),
        tile(16, 2),
        dma((12,)),
        dma((3,)), dma((3,)),
        dma((7,)), dma((7,)),
        dma((7,)), dma((7,)),
        dma((8,)), dma((8,)),
        dma((7,)), dma((7,)),
        dma((7,)), dma((7,)),
        dma((8,)), dma((8,)),
        dma((3,)), dma((3,)),
        dma((16,)), dma((16,)),
        pltpu.SemaphoreType.REGULAR((3,)),
    ]
    return pl.pallas_call(
        kernel,
        name="features",
        out_shape=jax.ShapeDtypeStruct((10, 16), F32),
        in_specs=[pl.BlockSpec(memory_space=pl.ANY)] * 12,
        out_specs=pl.BlockSpec(memory_space=pltpu.VMEM),
        scratch_shapes=scratch,
        compiler_params=pltpu.CompilerParams(
            collective_id=0, has_side_effects=True, vmem_limit_bytes=40 << 20
        ),
    )(
        xt.reshape(NT, HALF), ct.reshape(NT, HALF), lt,
        xv.reshape(NV, HALF), cv.reshape(NV, HALF), lv,
        ad, au, mom1, mom2, rank_p, feat_p,
    )


def solution(mesh):
    placed = (
        P("dp", None, "fsdp"),
        P("dp", None, "fsdp"),
        P("dp", None),
        P("dp", None, "fsdp"),
        P("dp", None, "fsdp"),
        P("dp", None),
        P(None, "fsdp"),
        P(None, "fsdp"),
        P(None, None, "fsdp"),
        P(None, None, "fsdp"),
        P(),
        P(None, "fsdp", None),
    )
    return jax.shard_map(
        body, mesh=mesh, in_specs=placed, out_specs=P("dp", "fsdp"), check_vma=False
    )
```

time: 602 us -> 63.9 us (0.11)
  waiting for transfers between devices: 438 us -> 0 us
  blocking collectives: 118 us -> 0 us
  Pallas kernels: 0 us -> 52.6 us
  matrix products: 20 us -> 0 us
  between operations: 13.3 us -> 0.04 us
    reduce_scatter x2 -> x0, waiting for transfers between devices: 189 us -> none  [the longest x1 99.8 us: body(): lax.psum_scatter(train_rows, 'fsdp', scatter_dimension=3, tiled=True)]
    psum x1 -> x0, waiting for transfers between devices: 162 us -> none  [body(): lax.psum((train_input_pair, validation_input_pair), 'fsdp')]
    unnamed x5 -> x0, waiting for transfers between devices: 87.7 us -> none
    all_gather x1 -> x0, blocking collectives: 83.4 us -> none  [body(): lax.all_gather(valid_unit, 'dp', axis=0, tiled=True)]
    pallas_call x0 -> x1, Pallas kernels: none -> 52.6 us  [body(): pl.pallas_call(kernel, name='features', out_shape=jax.ShapeDtypeStruct((1...]
    psum x1 -> x0, blocking collectives: 34.3 us -> none  [body(): lax.psum((jnp.sum(train_feat * train_feat, axis=(1, 2, 3)), jnp.sum(valid...]
    dot_general x13 -> x0, matrix products: 20 us -> none  [the longest x1 5.79 us: body(): jnp.einsum('eabk,vabk->ev', train_unit, lax.all_gather(valid_unit, 'dp',...]
    unnamed x23 -> x24, local copies, waits for them, and re-layouts: 1.42 us -> 10.7 us
  transfers between devices with their start and end apart: 4 -> 0, of which waited for: 4 -> 0; matrix products, arithmetic and copies ran while one was open for 1% -> 0% of each run, Pallas kernels for 0% -> 0%
where the time goes in v1:
time: 63.9 us; the launch traced here: 63.4 us
  Pallas kernels  52.6 us (82%)
  local copies, waits for them, and re-layouts  10.7 us (17%)
    pallas_call x1, Pallas kernels, body(): pl.pallas_call(kernel, name='features', out_shape=jax.ShapeDtypeStruct((1...  52.6 us
    unnamed x24, local copies, waits for them, and re-layouts  10.7 us

profile of v1, /device:TPU:1, one launch (start us, length us, event | category | flops | bytes accessed | tf_op | source)
XLA Modules:
  0.0 63.4 jit_solution(7587929444668147264)
XLA Ops:
  0.0 0.0 copy-start.9
  0.0 0.0 copy-start.10
  0.0 0.8 %copy.13.rank_p = bf16[2,64,16]{2,1,0:T(8,128)(2,1)S(1)} copy(bf16[2,64,16]{1,2,0:T(8,128)(2,1)} %param.22) | data formatting | bytes 8192 | tf_op args[10]
  0.8 0.0 copy-done.9
  0.8 0.0 copy-done.10
  0.8 0.0 copy-start
  0.9 1.2 %copy-done = bf16[10,96,512]{2,1,0:T(8,128)(2,1)S(1)} copy-done((bf16[10,96,512]{2,1,0:T(8,128)(2,1)S(1)}, bf16[10,96,512]{2,1,0:T(8,128)(2,1)}, u32[]{:S(2)}) %copy-start) | copy-done | bytes 983064
  2.0 0.0 copy-start.1
  2.0 1.2 %copy-done.1 = bf16[10,96,512]{2,1,0:T(8,128)(2,1)S(1)} copy-done((bf16[10,96,512]{2,1,0:T(8,128)(2,1)S(1)}, bf16[10,96,512]{2,1,0:T(8,128)(2,1)}, u32[]{:S(2)}) %copy-start.1) | copy-done | bytes 983064
  3.2 0.0 copy-start.2
  3.2 1.1 %copy-done.2 = bf16[8,96,512]{2,1,0:T(8,128)(2,1)S(1)} copy-done((bf16[8,96,512]{2,1,0:T(8,128)(2,1)S(1)}, bf16[8,96,512]{2,1,0:T(8,128)(2,1)}, u32[]{:S(2)}) %copy-start.2) | copy-done | bytes 786456
  4.4 0.0 copy-start.3
  4.4 1.1 %copy-done.3 = bf16[8,96,512]{2,1,0:T(8,128)(2,1)S(1)} copy-done((bf16[8,96,512]{2,1,0:T(8,128)(2,1)S(1)}, bf16[8,96,512]{2,1,0:T(8,128)(2,1)}, u32[]{:S(2)}) %copy-start.3) | copy-done | bytes 786456
  5.5 0.0 copy-start.4
  5.5 1.0 %copy-done.4 = bf16[2,512,256]{2,1,0:T(8,128)(2,1)S(1)} copy-done((bf16[2,512,256]{2,1,0:T(8,128)(2,1)S(1)}, bf16[2,512,256]{2,1,0:T(8,128)(2,1)}, u32[]{:S(2)}) %copy-start.4) | copy-done | bytes 524312
  6.6 0.0 copy-start.5
  6.6 0.9 %copy-done.5 = f32[2,64,512]{2,1,0:T(8,128)S(1)} copy-done((f32[2,64,512]{2,1,0:T(8,128)S(1)}, f32[2,64,512]{2,1,0:T(8,128)}, u32[]{:S(2)}) %copy-start.5) | copy-done | bytes 262168
  7.5 0.0 copy-start.6
  7.5 0.9 %copy-done.6 = f32[2,64,512]{2,1,0:T(8,128)S(1)} copy-done((f32[2,64,512]{2,1,0:T(8,128)S(1)}, f32[2,64,512]{2,1,0:T(8,128)}, u32[]{:S(2)}) %copy-start.6) | copy-done | bytes 262168
  8.5 0.0 copy-start.7
  8.5 0.8 %copy-done.7 = bf16[64,512]{1,0:T(8,128)(2,1)S(1)} copy-done((bf16[64,512]{1,0:T(8,128)(2,1)S(1)}, bf16[64,512]{1,0:T(8,128)(2,1)}, u32[]{:S(2)}) %copy-start.7) | copy-done | bytes 65560
  9.3 0.0 copy-start.8
  9.3 0.8 %copy-done.8 = bf16[64,512]{1,0:T(8,128)(2,1)S(1)} copy-done((bf16[64,512]{1,0:T(8,128)(2,1)S(1)}, bf16[64,512]{1,0:T(8,128)(2,1)}, u32[]{:S(2)}) %copy-start.8) | copy-done | bytes 65560
  10.1 52.6 %features.1 = f32[10,16]{1,0:T(8,128)S(1)} custom-call(bf16[960,512]{1,0:T(8,128)(2,1)S(1)} %bitcast.4, bf16[960,512]{1,0:T(8,128)(2,1)S(1)} %bitcast.5, s32[10,96]{1,0:T(8,128)S(1)} %copy-done.9, bf16[768,512]{1,0:T(8,128)(2,1)S(1)} %bitcast.6, bf16[768,512]{1,0:T(8,128)(2,1)S(1)} %bitcast.7, s32[8,96]{1,0:T(8,128)S(1)} %copy-done.10, ...), custom_call_target="tpu_custom_call" | custom-call | tf_op jit(solution)/shard_map/features/pallas_call | solution.py:487
  62.8 0.6 copy.15
Async XLA Ops:
  0.0 0.8 %copy-start.9 = (s32[10,96]{1,0:T(8,128)S(1)}, s32[10,96]{1,0:T(8,128)}, u32[]{:S(2)}) copy-start(s32[10,96]{1,0:T(8,128)} %lt.1) | copy-start | bytes 11524
  0.0 0.8 %copy-start.10 = (s32[8,96]{1,0:T(8,128)S(1)}, s32[8,96]{1,0:T(8,128)}, u32[]{:S(2)}) copy-start(s32[8,96]{1,0:T(8,128)} %lv.1) | copy-start | bytes 9220
  0.8 1.2 %copy-start = (bf16[10,96,512]{2,1,0:T(8,128)(2,1)S(1)}, bf16[10,96,512]{2,1,0:T(8,128)(2,1)}, u32[]{:S(2)}) copy-start(bf16[10,96,512]{2,1,0:T(8,128)(2,1)} %param.12) | copy-start | bytes 2949124
  2.0 1.2 %copy-start.1 = (bf16[10,96,512]{2,1,0:T(8,128)(2,1)S(1)}, bf16[10,96,512]{2,1,0:T(8,128)(2,1)}, u32[]{:S(2)}) copy-start(bf16[10,96,512]{2,1,0:T(8,128)(2,1)} %param.13) | copy-start | bytes 2949124
  3.2 1.1 %copy-start.2 = (bf16[8,96,512]{2,1,0:T(8,128)(2,1)S(1)}, bf16[8,96,512]{2,1,0:T(8,128)(2,1)}, u32[]{:S(2)}) copy-start(bf16[8,96,512]{2,1,0:T(8,128)(2,1)} %param.15) | copy-start | bytes 2359300
  4.4 1.1 %copy-start.3 = (bf16[8,96,512]{2,1,0:T(8,128)(2,1)S(1)}, bf16[8,96,512]{2,1,0:T(8,128)(2,1)}, u32[]{:S(2)}) copy-start(bf16[8,96,512]{2,1,0:T(8,128)(2,1)} %param.16) | copy-start | bytes 2359300
  5.5 1.0 %copy-start.4 = (bf16[2,512,256]{2,1,0:T(8,128)(2,1)S(1)}, bf16[2,512,256]{2,1,0:T(8,128)(2,1)}, u32[]{:S(2)}) copy-start(bf16[2,512,256]{2,1,0:T(8,128)(2,1)} %feat_p.1) | copy-start | bytes 1572868
  6.6 0.9 %copy-start.5 = (f32[2,64,512]{2,1,0:T(8,128)S(1)}, f32[2,64,512]{2,1,0:T(8,128)}, u32[]{:S(2)}) copy-start(f32[2,64,512]{2,1,0:T(8,128)} %mom1.1) | copy-start | bytes 786436
  7.5 0.9 %copy-start.6 = (f32[2,64,512]{2,1,0:T(8,128)S(1)}, f32[2,64,512]{2,1,0:T(8,128)}, u32[]{:S(2)}) copy-start(f32[2,64,512]{2,1,0:T(8,128)} %mom2.1) | copy-start | bytes 786436
  8.5 0.8 %copy-start.7 = (bf16[64,512]{1,0:T(8,128)(2,1)S(1)}, bf16[64,512]{1,0:T(8,128)(2,1)}, u32[]{:S(2)}) copy-start(bf16[64,512]{1,0:T(8,128)(2,1)} %ad.1) | copy-start | bytes 196612
  9.3 0.8 %copy-start.8 = (bf16[64,512]{1,0:T(8,128)(2,1)S(1)}, bf16[64,512]{1,0:T(8,128)(2,1)}, u32[]{:S(2)}) copy-start(bf16[64,512]{1,0:T(8,128)(2,1)} %au.1) | copy-start | bytes 196612

commit v2 on v1

--- a/solution.py
+++ b/solution.py
@@ -99,14 +99,14 @@
             device_id=peer, device_id_type=MESH,
         )
 
+    def arrived(src, dst, sem):
+        pltpu.make_async_copy(src, dst, sem).wait()
+
     lane = lax.broadcasted_iota(jnp.int32, (16, 128), 1)
 
     def inner(c, at):
         wc = w[c]
-        proj = lax.dot_general(
-            rp[c], wc, (((0,), (0,)), ((), ())), preferred_element_type=F32
-        )
-        hi, lo = split(proj)
+        hi, lo = split(dot(rp[c], wc))
         both = jnp.concatenate([hi, lo], axis=0)
         for t in range(4):
             o = dot_nt(wc, buf[c, pl.ds(256 * t, 256), :])
@@ -176,9 +176,9 @@
     in2 = (iota((32, 128), 0) & 1) == lax.shift_right_logical(iota((32, 128), 1), 6)
     for c in range(2):
         pc = rp[c]
-        a8 = dot(dot_nt(up8, pc).astype(BF16), wide)
+        a8 = dot(dot(up8, pc).astype(BF16), wide)
         pm8[c] = jnp.where(in8, a8, 0.0).astype(BF16)
-        a2 = dot(dot_nt(up2, pc).astype(BF16), wide[:, :128])
+        a2 = dot(dot(up2, pc).astype(BF16), wide[:, :128])
         pm2[c] = jnp.where(in2, a2, 0.0).astype(BF16)
 
     pl.semaphore_wait(tok.at[0], 2)
@@ -362,7 +362,7 @@
     for cp in q_t:
         cp.start()
     for i in range(8):
-        pltpu.make_async_copy(vs, vg.at[i], r_c.at[i]).wait()
+        arrived(vs, vg.at[i], r_c.at[i])
     vals = jnp.concatenate([vg[:, t].reshape(64, 128) for t in range(4)], axis=1)
     ones = jnp.ones((8, HALF), F32)
     nv = dot_nt(ones, vals * vals, lax.Precision.HIGHEST)
@@ -416,7 +416,7 @@
         c_v[7].wait_send()
 
     for i in range(16):
-        pltpu.make_async_copy(ds.at[0], dr.at[i], r_d.at[i]).wait()
+        arrived(ds.at[0], dr.at[i], r_d.at[i])
     sa = dr[0, 0]
     sb = dr[0, 1]
     for i in range(1, 16):
@@ -445,7 +445,7 @@
     scratch = [
         pltpu.VMEM((2, NT + NV, HALF), BF16),
         pltpu.VMEM((2, 64, HALF), BF16),
-        pltpu.VMEM((2, 64, 16), BF16),
+        pltpu.VMEM((2, 16, 64), BF16),
         pltpu.VMEM((2, HALF, 256), BF16),
         pltpu.VMEM((2, 64, HALF), F32),
         pltpu.VMEM((2, 64, HALF), F32),
@@ -488,16 +488,16 @@
         kernel,
         name="features",
         out_shape=jax.ShapeDtypeStruct((10, 16), F32),
-        in_specs=[pl.BlockSpec(memory_space=pl.ANY)] * 12,
+        in_specs=[pl.BlockSpec(memory_space=pltpu.HBM)] * 12,
         out_specs=pl.BlockSpec(memory_space=pltpu.VMEM),
         scratch_shapes=scratch,
         compiler_params=pltpu.CompilerParams(
-            collective_id=0, has_side_effects=True, vmem_limit_bytes=40 << 20
+            collective_id=0, has_side_effects=True, vmem_limit_bytes=60 << 20
         ),
     )(
         xt.reshape(NT, HALF), ct.reshape(NT, HALF), lt,
         xv.reshape(NV, HALF), cv.reshape(NV, HALF), lv,
-        ad, au, mom1, mom2, rank_p, feat_p,
+        ad, au, mom1, mom2, jnp.swapaxes(rank_p, 1, 2), feat_p,
     )
 
 

time: 63.9 us -> 54 us (0.85)
  local copies, waits for them, and re-layouts: 10.7 us -> 1.3 us
    unnamed x24 -> x1, local copies, waits for them, and re-layouts: 10.7 us -> 1.3 us
where the time goes in v2:
time: 54 us; the launch traced here: 53.8 us
  Pallas kernels  52.5 us (97%)
  local copies, waits for them, and re-layouts  1.3 us (2%)
    pallas_call x1, Pallas kernels, body(): pl.pallas_call(kernel, name='features', out_shape=jax.ShapeDtypeStruct((1...  52.5 us
    unnamed x1, local copies, waits for them, and re-layouts  1.3 us

profile of v2, /device:TPU:1, one launch (start us, length us, event | category | flops | bytes accessed | tf_op | source)
XLA Modules:
  0.0 53.8 jit_solution(6303999178898363297)
XLA Ops:
  0.0 52.5 %features.1 = f32[10,16]{1,0:T(8,128)} custom-call(bf16[960,512]{1,0:T(8,128)(2,1)} %bitcast.5, bf16[960,512]{1,0:T(8,128)(2,1)} %bitcast.6, s32[10,96]{1,0:T(8,128)} %lt.1, bf16[768,512]{1,0:T(8,128)(2,1)} %bitcast.7, bf16[768,512]{1,0:T(8,128)(2,1)} %bitcast.8, s32[8,96]{1,0:T(8,128)} %lv.1, bf16[64,512]{1,0:T(8,128)(2,1)} %ad.1, bf16[64,512]{1,0:T(8,128)(2,1)} %au.1, ...), custom_call_target="tpu_custom_call" | custom-call | tf_op jit(solution)/shard_map/features/pallas_call | solution.py:487
  52.5 1.3 %copy.14 = f32[10,16]{1,0:T(8,128)} copy(f32[10,16]{1,0:T(8,128)} %features.1) | data formatting | bytes 1280

commit v3 on v2

--- a/solution.py
+++ b/solution.py
@@ -42,9 +42,10 @@
     xt, ct, lt, xv, cv, lv, ad, au, mom1, mom2, rank_p, feat_p,
     out,
     buf, w, rp, fp, m_, v_, labt, labv,
-    zp, ztw, ar, zf, wt, bd, pm8, pm2, dirs,
+    zv, zvtw, arv, zfv, zt, zttw, art, zft, wt, bd, pm8, pm2, dirs,
     pvl, pvtw, bvr, ptl, pttw, btr, vs, ts, vg, tg, ds, dr,
-    ld, s_tw, r_tw, s_a1, r_a1, s_a2, r_a2, s_fw, r_fw, s_bv, r_bv, s_bt, r_bt,
+    ld, la, s_tw, r_tw, s_a1v, r_a1v, s_a2v, r_a2v, s_fwv, r_fwv,
+    s_a1t, r_a1t, s_a2t, r_a2t, s_fwt, r_fwt, s_bv, r_bv, s_bt, r_bt,
     s_c, r_c, s_q, r_q, s_d, r_d, tok,
 ):
     d = lax.axis_index("dp")
@@ -67,31 +68,59 @@
     def z_off(n):
         return dp_at(y, lax.rem(z + n + 16, 16))
 
-    loads = [
+    barrier = pltpu.get_barrier_semaphore()
+    zo = z + 1 - 2 * zr
+    greet = [(d, to * 2 + k) for to, _ in chips]
+    greet += [twin, (dp_at(1 - y, z), f), (dp_at(y, zo), f), (dp_at(1 - y, zo), f)]
+    greet += [(dp_at(y, lax.rem(z + 15 + 2 * zr, 16)), f)]
+    for peer in greet:
+        pl.semaphore_signal(barrier, inc=1, device_id=peer, device_id_type=MESH)
+
+    last = 896
+    loads = (
         (au, w.at[0]),
         (ad, w.at[1]),
         (rank_p, rp),
-        (ct, buf.at[0, pl.ds(0, NT)]),
-        (cv, buf.at[0, pl.ds(NT, NV)]),
-        (xt, buf.at[1, pl.ds(0, NT)]),
-        (xv, buf.at[1, pl.ds(NT, NV)]),
         (lt, labt),
         (lv, labv),
         (feat_p, fp),
         (mom1, m_),
         (mom2, v_),
-    ]
+    )
     load = [pltpu.make_async_copy(a, b, ld.at[i]) for i, (a, b) in enumerate(loads)]
-    for cp in load:
+    acts = []
+    for c, (tr, va) in enumerate(((ct, cv), (xt, xv))):
+        acts.append(
+            [
+                pltpu.make_async_copy(a, buf.at[c, pl.ds(to, n)], la.at[c, i])
+                for i, (a, to, n) in enumerate(
+                    (
+                        (va, NT, NV),
+                        (tr.at[pl.ds(last, NT - last)], last, NT - last),
+                        (tr.at[pl.ds(0, last)], 0, last),
+                    )
+                )
+            ]
+        )
+    for cp in load[:3]:
         cp.start()
-
-    barrier = pltpu.get_barrier_semaphore()
-    zt = z + 1 - 2 * zr
-    greet = [(d, to * 2 + k) for to, _ in chips]
-    greet += [twin, (dp_at(1 - y, z), f), (dp_at(y, zt), f), (dp_at(1 - y, zt), f)]
-    greet += [(dp_at(y, lax.rem(z + 15 + 2 * zr, 16)), f)]
-    for peer in greet:
-        pl.semaphore_signal(barrier, inc=1, device_id=peer, device_id_type=MESH)
+    for mine_k in range(2):
+
+        @pl.when(k == mine_k)
+        def _():
+            for i in (0, 1, 2):
+                for c in (1 - mine_k, mine_k):
+                    acts[c][i].start()
+
+    for cp in load[3:]:
+        cp.start()
+
+    def loaded(c, i):
+        src = xt.at[pl.ds(0, (NV, NT - last, last)[i])] if i else xv
+        at = (NT, last, 0)[i]
+        pltpu.make_async_copy(
+            src, buf.at[c, pl.ds(at, (NV, NT - last, last)[i])], la.at[c, i]
+        ).wait()
 
     def remote(src, dst, send, recv, peer):
         return pltpu.make_async_remote_copy(
@@ -104,17 +133,11 @@
 
     lane = lax.broadcasted_iota(jnp.int32, (16, 128), 1)
 
-    def inner(c, at):
+    def inner_valid(c, at):
         wc = w[c]
         hi, lo = split(dot(rp[c], wc))
         both = jnp.concatenate([hi, lo], axis=0)
-        for t in range(4):
-            o = dot_nt(wc, buf[c, pl.ds(256 * t, 256), :])
-            zp[at, :, 2 * t] = o[:, :128].reshape(8, 8, 128)
-            if t < 3:
-                zp[at, :, 2 * t + 1] = o[:, 128:].reshape(8, 8, 128)
-            else:
-                tail = o[:, 128:]
+        tail = dot_nt(wc, buf[c, pl.ds(last, 128), :])
         for g in range(4):
             rows = jnp.concatenate(
                 [
@@ -125,30 +148,56 @@
             )
             o = dot_nt(both, rows)
             o = o[:16] + o[16:]
-            zp[at, 2 * g : 2 * g + 2, 8] = o[:, :128].reshape(2, 8, 128)
+            zv[at, 2 * g : 2 * g + 2, 1] = o[:, :128].reshape(2, 8, 128)
             mixed = jnp.where(lane < 64, tail[16 * g : 16 * g + 16], o[:, 128:])
-            zp[at, 2 * g : 2 * g + 2, 7] = mixed.reshape(2, 8, 128)
-
-    for i in range(7):
+            zv[at, 2 * g : 2 * g + 2, 0] = mixed.reshape(2, 8, 128)
+
+    def inner_train(c, at):
+        wc = w[c]
+        for t in range(4):
+            n = 256 if t < 3 else 128
+            o = dot_nt(wc, buf[c, pl.ds(256 * t, n), :])
+            for j in range(n // 128):
+                zt[at, :, 2 * t + j] = o[:, 128 * j : 128 * j + 128].reshape(8, 8, 128)
+
+    def to_chips(src, dst, send, recv):
+        cps = [
+            remote(src(to), dst(i), send.at[i], recv.at[i], (d, to * 2 + k))
+            for i, (to, _) in enumerate(chips)
+        ]
+        for cp in cps:
+            cp.start()
+        return cps
+
+    for i in range(3):
         load[i].wait()
-    inner(other, 0)
-    pl.semaphore_wait(barrier, len(greet))
-    tw_a = remote(zp.at[0], ztw, s_tw.at[0], r_tw.at[0], twin)
-    tw_a.start()
-    for n in (-1, 1):
-        pl.semaphore_signal(tok.at[0], inc=1, device_id=(z_off(n), f), device_id_type=MESH)
-    inner(k, 1)
-    tw_a.wait_recv()
-    zp[1] = zp[1] + ztw[...]
-    a1 = [
-        remote(zp.at[1, to], ar.at[i], s_a1.at[i], r_a1.at[i], (d, to * 2 + k))
-        for i, (to, _) in enumerate(chips)
-    ]
-    for cp in a1:
-        cp.start()
-
-    for i in range(7, 12):
-        load[i].wait()
+    for c in (other, k):
+        loaded(c, 0)
+        loaded(c, 1)
+        inner_valid(c, 0) if c is other else inner_valid(c, 1)
+        if c is other:
+            pl.semaphore_wait(barrier, len(greet))
+            tw_av = remote(zv.at[0], zvtw, s_tw.at[0], r_tw.at[0], twin)
+            tw_av.start()
+            for n in (-1, 1):
+                pl.semaphore_signal(
+                    tok.at[0], inc=1, device_id=(z_off(n), f), device_id_type=MESH
+                )
+    loaded(other, 2)
+    inner_train(other, 0)
+    tw_at = remote(zt.at[0], zttw, s_tw.at[3], r_tw.at[3], twin)
+    tw_at.start()
+    tw_av.wait_recv()
+    zv[1] = zv[1] + zvtw[...]
+    a1v = to_chips(lambda to: zv.at[1, to], lambda i: arv.at[i], s_a1v, r_a1v)
+    loaded(k, 2)
+    inner_train(k, 1)
+    tw_at.wait_recv()
+    zt[1] = zt[1] + zttw[...]
+    a1t = to_chips(lambda to: zt.at[1, to], lambda i: art.at[i], s_a1t, r_a1t)
+
+    for cp in load[3:]:
+        cp.wait()
     iota = lambda shape, dim: lax.broadcasted_iota(jnp.int32, shape, dim)
     one = lambda cond: jnp.where(cond, 1.0, 0.0)
     tl = iota((1, 1024), 1)
@@ -185,34 +234,48 @@
     for n in (-2, 2):
         pl.semaphore_signal(tok.at[1], inc=1, device_id=(z_off(n), f), device_id_type=MESH)
 
-    total = zp[1, q]
-    for i in reversed(range(7)):
-        a1[i].wait_recv()
-        total = total + ar[i]
-    zf[k, q] = total
-    a2 = [
-        remote(zf.at[k, q], zf.at[k, q], s_a2.at[i], r_a2.at[i], (d, to * 2 + k))
-        for i, (to, _) in enumerate(chips)
-    ]
-    for cp in a2:
+    def summed(own, cps, parts):
+        total = own
+        for i in reversed(range(7)):
+            cps[i].wait_recv()
+            total = total + parts[i]
+        return total
+
+    def spread_out(zf, send, recv, fsend, frecv):
+        cps = to_chips(lambda to: zf.at[k, q], lambda i: zf.at[k, q], send, recv)
+        cp = remote(zf.at[k, q], zf.at[k, q], fsend.at[7], frecv.at[7], twin)
         cp.start()
-    fw = [None] * 8
-    fw[7] = remote(zf.at[k, q], zf.at[k, q], s_fw.at[7], r_fw.at[7], twin)
-    fw[7].start()
+        return cps + [cp]
+
+    def forward(zf, send, recv, fsend, frecv):
+        cps = []
+        for i in reversed(range(7)):
+            fro = chips[i][1]
+            at = zf.at[k, fro]
+            remote(at, at, send.at[i], recv.at[i], twin).wait_recv()
+            cps.append(remote(at, at, fsend.at[i], frecv.at[i], twin))
+            cps[-1].start()
+        return cps
+
+    def forwarded(zf, fsend, frecv):
+        for i in range(8):
+            at = zf.at[other, q if i == 7 else chips[i][1]]
+            remote(at, at, fsend.at[i], frecv.at[i], twin).wait_recv()
+
+    zfv[k, q] = summed(zv[1, q], a1v, arv)
+    a2v = spread_out(zfv, s_a2v, r_a2v, s_fwv, r_fwv)
+    zft[k, q] = summed(zt[1, q], a1t, art)
+    a2t = spread_out(zft, s_a2t, r_a2t, s_fwt, r_fwt)
     pl.semaphore_wait(tok.at[1], 2)
     for n in (-4, 4):
         pl.semaphore_signal(tok.at[2], inc=1, device_id=(z_off(n), f), device_id_type=MESH)
-    for i in reversed(range(7)):
-        fro = chips[i][1]
-        remote(zf.at[k, fro], zf.at[k, fro], s_a2.at[i], r_a2.at[i], twin).wait_recv()
-        fw[i] = remote(zf.at[k, fro], zf.at[k, fro], s_fw.at[i], r_fw.at[i], twin)
-        fw[i].start()
+    a2v += forward(zfv, s_a2v, r_a2v, s_fwv, r_fwv)
 
     def valid_features(c, at):
         lhs, rhs = [], []
         for g in range(4):
-            za = zf[c, 2 * g : 2 * g + 2, 8].reshape(16, 128)
-            zb = zf[c, 2 * g : 2 * g + 2, 7].reshape(16, 128)
+            za = zfv[c, 2 * g : 2 * g + 2, 1].reshape(16, 128)
+            zb = zfv[c, 2 * g : 2 * g + 2, 0].reshape(16, 128)
             zg = jnp.concatenate([za, zb], axis=1)
             hi = zg.astype(BF16).astype(F32)
             lo = zg - hi
@@ -248,9 +311,8 @@
 
     def train_pair(c, i):
         t0 = (192 * i) // 128
-        zg = jnp.concatenate(
-            [zf[c, :, t0].reshape(64, 128), zf[c, :, t0 + 1].reshape(64, 128)], axis=1
-        )
+        second = zft[c, :, t0 + 1] if t0 < 6 else zfv[c, :, 0]
+        zg = jnp.concatenate([zft[c, :, t0].reshape(64, 128), second.reshape(64, 128)], axis=1)
         cols = pl.ds(128 * t0, 256)
         lhs = jnp.concatenate(
             [zg * wt[2 * i : 2 * i + 1, cols], zg * wt[2 * i + 1 : 2 * i + 2, cols]], axis=0
@@ -282,28 +344,26 @@
                 ptl[at, p, 4, pl.ds(4 * h, 4), :] = cols[128 + 4 * p : 132 + 4 * p]
 
     valid_features(k, 1)
-    for i in range(8):
-        at = q if i == 7 else chips[i][1]
-        remote(
-            zf.at[other, at], zf.at[other, at], s_fw.at[i], r_fw.at[i], twin
-        ).wait_recv()
+    forwarded(zfv, s_fwv, r_fwv)
     valid_features(other, 0)
     tw_v = remote(pvl.at[0], pvtw, s_tw.at[1], r_tw.at[1], twin)
     tw_v.start()
+    tw_v.wait_recv()
+    pvl[1] = pvl[1] + pvtw[...]
+    b_v = to_chips(lambda to: pvl.at[1, to], lambda i: bvr.at[i], s_bv, r_bv)
+    a2t += forward(zft, s_a2t, r_a2t, s_fwt, r_fwt)
+    forwarded(zft, s_fwt, r_fwt)
     for i in range(5):
         train_pair(other, i)
-        if i == 1:
-            tw_v.wait_recv()
-            pvl[1] = pvl[1] + pvtw[...]
-            b_v = [
-                remote(pvl.at[1, to], bvr.at[j], s_bv.at[j], r_bv.at[j], (d, to * 2 + k))
-                for j, (to, _) in enumerate(chips)
-            ]
-            for cp in b_v:
-                cp.start()
     train_features(other, 0)
     tw_t = remote(ptl.at[0], pttw, s_tw.at[2], r_tw.at[2], twin)
     tw_t.start()
+    for i in range(5):
+        train_pair(k, i)
+    train_features(k, 1)
+    tw_t.wait_recv()
+    ptl[1] = ptl[1] + pttw[...]
+    b_t = to_chips(lambda to: ptl.at[1, to], lambda i: btr.at[i], s_bt, r_bt)
 
     par = lax.rem(zm, 2)
     slot = lax.div(zm, 2) * 2 + zr
@@ -314,46 +374,27 @@
         c_v.append(remote(vs, vg.at[slot], s_c.at[j], r_c.at[slot], peer))
     keep_v = pltpu.make_async_copy(vs, vg.at[slot], r_c.at[slot])
 
-    for i in range(5):
-        train_pair(k, i)
-        if i == 2:
-            pl.semaphore_wait(tok.at[2], 2)
-            total = pvl[1, q]
-            for j in reversed(range(7)):
-                b_v[j].wait_recv()
-                total = total + bvr[j]
-            vs[...] = total
-            for cp in c_v[:7]:
-                cp.start()
-
-            @pl.when(mine)
-            def _():
-                keep_v.start()
-
-            @pl.when(jnp.logical_not(mine))
-            def _():
-                c_v[7].start()
-
-    train_features(k, 1)
-    tw_t.wait_recv()
-    ptl[1] = ptl[1] + pttw[...]
-    b_t = [
-        remote(ptl.at[1, to], btr.at[j], s_bt.at[j], r_bt.at[j], (d, to * 2 + k))
-        for j, (to, _) in enumerate(chips)
-    ]
-    for cp in b_t:
+    pl.semaphore_wait(tok.at[2], 2)
+    vs[...] = summed(pvl[1, q], b_v, bvr)
+    for cp in c_v[:7]:
         cp.start()
-    total = ptl[1, q]
-    for j in reversed(range(7)):
-        b_t[j].wait_recv()
-        total = total + btr[j]
+
+    @pl.when(mine)
+    def _():
+        keep_v.start()
+
+    @pl.when(jnp.logical_not(mine))
+    def _():
+        c_v[7].start()
+
+    total = summed(ptl[1, q], b_t, btr)
     ts[...] = total
     blk = 2 * y + zr
     tg[blk] = total
     partners = (
-        (1 - y, zt, 2 * (1 - y) + 1 - zr),
+        (1 - y, zo, 2 * (1 - y) + 1 - zr),
         (1 - y, z, 2 * (1 - y) + zr),
-        (y, zt, 2 * y + 1 - zr),
+        (y, zo, 2 * y + 1 - zr),
     )
     q_t = [
         remote(ts, tg.at[blk], s_q.at[j], r_q.at[j], (dp_at(py, pz), f))
@@ -408,7 +449,7 @@
                 def _():
                     keep.start()
 
-    for cp in [tw_a, tw_v, tw_t] + a1 + a2 + fw + b_v + b_t + c_v[:7] + q_t:
+    for cp in [tw_av, tw_at, tw_v, tw_t] + a1v + a1t + a2v + a2t + b_v + b_t + c_v[:7] + q_t:
         cp.wait_send()
 
     @pl.when(jnp.logical_not(mine))
@@ -451,10 +492,14 @@
         pltpu.VMEM((2, 64, HALF), F32),
         pltpu.VMEM((10, SEG), jnp.int32),
         pltpu.VMEM((8, SEG), jnp.int32),
-        tile(2, 8, 9),
-        tile(8, 9),
-        tile(7, 9),
-        tile(2, 8, 9),
+        tile(2, 8, 2),
+        tile(8, 2),
+        tile(7, 2),
+        tile(2, 8, 2),
+        tile(2, 8, 7),
+        tile(8, 7),
+        tile(7, 7),
+        tile(2, 8, 7),
         pltpu.VMEM((16, 1024), F32),
         pltpu.VMEM((8, 1024), F32),
         pltpu.VMEM((2, 128, HALF), BF16),
@@ -472,8 +517,12 @@
         tile(4, 5),
         tile(4, 2),
         tile(16, 2),
-        dma((12,)),
-        dma((3,)), dma((3,)),
+        dma((8,)),
+        dma((2, 3)),
+        dma((4,)), dma((4,)),
+        dma((7,)), dma((7,)),
+        dma((7,)), dma((7,)),
+        dma((8,)), dma((8,)),
         dma((7,)), dma((7,)),
         dma((7,)), dma((7,)),
         dma((8,)), dma((8,)),

time: 54 us -> 51.6 us (0.956)
  Pallas kernels: 52.5 us -> 50.2 us
    pallas_call x1, Pallas kernels: 52.5 us -> 50.2 us  [body(): pl.pallas_call(kernel, name='features', out_shape=jax.ShapeDtypeStruct((1...]
where the time goes in v3:
time: 51.6 us; the launch traced here: 51.5 us
  Pallas kernels  50.2 us (97%)
  local copies, waits for them, and re-layouts  1.3 us (3%)
    pallas_call x1, Pallas kernels, body(): pl.pallas_call(kernel, name='features', out_shape=jax.ShapeDtypeStruct((1...  50.2 us
    unnamed x1, local copies, waits for them, and re-layouts  1.3 us

profile of v3, /device:TPU:1, one launch (start us, length us, event | category | flops | bytes accessed | tf_op | source)
XLA Modules:
  0.0 51.5 jit_solution(17811663435426792749)
XLA Ops:
  0.0 50.2 %features.1 = f32[10,16]{1,0:T(8,128)} custom-call(bf16[960,512]{1,0:T(8,128)(2,1)} %bitcast.5, bf16[960,512]{1,0:T(8,128)(2,1)} %bitcast.6, s32[10,96]{1,0:T(8,128)} %lt.1, bf16[768,512]{1,0:T(8,128)(2,1)} %bitcast.7, bf16[768,512]{1,0:T(8,128)(2,1)} %bitcast.8, s32[8,96]{1,0:T(8,128)} %lv.1, bf16[64,512]{1,0:T(8,128)(2,1)} %ad.1, bf16[64,512]{1,0:T(8,128)(2,1)} %au.1, ...), custom_call_target="tpu_custom_call" | custom-call | tf_op jit(solution)/shard_map/features/pallas_call | solution.py:536
  50.2 1.3 %copy.14 = f32[10,16]{1,0:T(8,128)} copy(f32[10,16]{1,0:T(8,128)} %features.1) | data formatting | bytes 1280

commit v4 on v3

--- a/solution.py
+++ b/solution.py
@@ -183,13 +183,13 @@
                 pl.semaphore_signal(
                     tok.at[0], inc=1, device_id=(z_off(n), f), device_id_type=MESH
                 )
+    tw_av.wait_recv()
+    zv[1] = zv[1] + zvtw[...]
+    a1v = to_chips(lambda to: zv.at[1, to], lambda i: arv.at[i], s_a1v, r_a1v)
     loaded(other, 2)
     inner_train(other, 0)
     tw_at = remote(zt.at[0], zttw, s_tw.at[3], r_tw.at[3], twin)
     tw_at.start()
-    tw_av.wait_recv()
-    zv[1] = zv[1] + zvtw[...]
-    a1v = to_chips(lambda to: zv.at[1, to], lambda i: arv.at[i], s_a1v, r_a1v)
     loaded(k, 2)
     inner_train(k, 1)
     tw_at.wait_recv()
@@ -456,6 +456,12 @@
     def _():
         c_v[7].wait_send()
 
+    for cp, here in d_c:
+
+        @pl.when(jnp.logical_not(here))
+        def _():
+            cp.wait_send()
+
     for i in range(16):
         arrived(ds.at[0], dr.at[i], r_d.at[i])
     sa = dr[0, 0]
@@ -473,11 +479,6 @@
         for i in range(1, 4):
             o = jnp.where(pick == i, res[:, 16 * i : 16 * i + 16], o)
         out[rows, :] = o
-    for cp, here in d_c:
-
-        @pl.when(jnp.logical_not(here))
-        def _():
-            cp.wait_send()
 
 
 def body(xt, ct, lt, xv, cv, lv, ad, au, mom1, mom2, rank_p, feat_p):
@@ -536,7 +537,7 @@
     return pl.pallas_call(
         kernel,
         name="features",
-        out_shape=jax.ShapeDtypeStruct((10, 16), F32),
+        out_shape=pltpu.VMEM((10, 16), F32),
         in_specs=[pl.BlockSpec(memory_space=pltpu.HBM)] * 12,
         out_specs=pl.BlockSpec(memory_space=pltpu.VMEM),
         scratch_shapes=scratch,

time: 51.6 us -> 49.7 us (0.963)
  Pallas kernels: 50.2 us -> 48.9 us
  local copies, waits for them, and re-layouts: 1.3 us -> 0.6 us
    pallas_call x1, Pallas kernels: 50.2 us -> 48.9 us  [body(): pl.pallas_call(kernel, name='features', out_shape=pltpu.VMEM((10, 16), F3...]
    unnamed x1, local copies, waits for them, and re-layouts: 1.3 us -> 0.6 us
where the time goes in v4:
time: 49.7 us; the launch traced here: 49.6 us
  Pallas kernels  48.9 us (98%)
  local copies, waits for them, and re-layouts  0.6 us (1%)
    pallas_call x1, Pallas kernels, body(): pl.pallas_call(kernel, name='features', out_shape=pltpu.VMEM((10, 16), F3...  48.9 us

profile of v4, /device:TPU:1, one launch (start us, length us, event | category | flops | bytes accessed | tf_op | source)
XLA Modules:
  0.0 49.6 jit_solution(17799064756926179146)
XLA Ops:
  0.0 48.9 %features.1 = f32[10,16]{1,0:T(8,128)S(1)} custom-call(bf16[960,512]{1,0:T(8,128)(2,1)} %bitcast.5, bf16[960,512]{1,0:T(8,128)(2,1)} %bitcast.6, s32[10,96]{1,0:T(8,128)} %lt.1, bf16[768,512]{1,0:T(8,128)(2,1)} %bitcast.7, bf16[768,512]{1,0:T(8,128)(2,1)} %bitcast.8, s32[8,96]{1,0:T(8,128)} %lv.1, bf16[64,512]{1,0:T(8,128)(2,1)} %ad.1, bf16[64,512]{1,0:T(8,128)(2,1)} %au.1, ...), custom_call_target="tpu_custom_call" | custom-call | tf_op jit(solution)/shard_map/features/pallas_call | solution.py:537
  49.0 0.6 %copy.14 = f32[10,16]{1,0:T(8,128)} copy(f32[10,16]{1,0:T(8,128)S(1)} %features.1) | data formatting | bytes 1280

commit v5 on v4

--- a/solution.py
+++ b/solution.py
@@ -161,13 +161,8 @@
                 zt[at, :, 2 * t + j] = o[:, 128 * j : 128 * j + 128].reshape(8, 8, 128)
 
     def to_chips(src, dst, send, recv):
-        cps = [
-            remote(src(to), dst(i), send.at[i], recv.at[i], (d, to * 2 + k))
-            for i, (to, _) in enumerate(chips)
-        ]
-        for cp in cps:
-            cp.start()
-        return cps
+        for i, (to, _) in enumerate(chips):
+            remote(src(to), dst(i), send, recv, (d, to * 2 + k)).start()
 
     for i in range(3):
         load[i].wait()
@@ -185,7 +180,7 @@
                 )
     tw_av.wait_recv()
     zv[1] = zv[1] + zvtw[...]
-    a1v = to_chips(lambda to: zv.at[1, to], lambda i: arv.at[i], s_a1v, r_a1v)
+    to_chips(lambda to: zv.at[1, to], lambda i: arv.at[i], s_a1v, r_a1v)
     loaded(other, 2)
     inner_train(other, 0)
     tw_at = remote(zt.at[0], zttw, s_tw.at[3], r_tw.at[3], twin)
@@ -194,7 +189,7 @@
     inner_train(k, 1)
     tw_at.wait_recv()
     zt[1] = zt[1] + zttw[...]
-    a1t = to_chips(lambda to: zt.at[1, to], lambda i: art.at[i], s_a1t, r_a1t)
+    to_chips(lambda to: zt.at[1, to], lambda i: art.at[i], s_a1t, r_a1t)
 
     for cp in load[3:]:
         cp.wait()
@@ -234,42 +229,36 @@
     for n in (-2, 2):
         pl.semaphore_signal(tok.at[1], inc=1, device_id=(z_off(n), f), device_id_type=MESH)
 
-    def summed(own, cps, parts):
+    def summed(own, parts, recv):
+        arrived(parts, parts, recv)
         total = own
-        for i in reversed(range(7)):
-            cps[i].wait_recv()
+        for i in range(7):
             total = total + parts[i]
         return total
 
-    def spread_out(zf, send, recv, fsend, frecv):
-        cps = to_chips(lambda to: zf.at[k, q], lambda i: zf.at[k, q], send, recv)
-        cp = remote(zf.at[k, q], zf.at[k, q], fsend.at[7], frecv.at[7], twin)
-        cp.start()
-        return cps + [cp]
-
-    def forward(zf, send, recv, fsend, frecv):
-        cps = []
-        for i in reversed(range(7)):
-            fro = chips[i][1]
-            at = zf.at[k, fro]
-            remote(at, at, send.at[i], recv.at[i], twin).wait_recv()
-            cps.append(remote(at, at, fsend.at[i], frecv.at[i], twin))
-            cps[-1].start()
-        return cps
-
-    def forwarded(zf, fsend, frecv):
-        for i in range(8):
-            at = zf.at[other, q if i == 7 else chips[i][1]]
-            remote(at, at, fsend.at[i], frecv.at[i], twin).wait_recv()
-
-    zfv[k, q] = summed(zv[1, q], a1v, arv)
-    a2v = spread_out(zfv, s_a2v, r_a2v, s_fwv, r_fwv)
-    zft[k, q] = summed(zt[1, q], a1t, art)
-    a2t = spread_out(zft, s_a2t, r_a2t, s_fwt, r_fwt)
+    def spread_out(zf, send, recv):
+        for i, (dx, _) in enumerate(OFFSETS):
+            at = zf.at[k, q]
+            remote(at, at, send, recv.at[dx], (d, chips[i][0] * 2 + k)).start()
+
+    def forward(zf, recv, fsend, frecv):
+        for dx in (0, 1, 3, 2):
+            pair = zf.at[k, pl.ds(2 * lax.rem(x + 4 - dx, 4), 2)]
+            come = pair if dx else zf.at[k, pl.ds(2 * x + 1 - yh, 1)]
+            arrived(come, come, recv.at[dx])
+            remote(pair, pair, fsend, frecv, twin).start()
+
+    def forwarded(zf, frecv):
+        arrived(zf.at[other], zf.at[other], frecv)
+
+    zfv[k, q] = summed(zv[1, q], arv, r_a1v)
+    spread_out(zfv, s_a2v, r_a2v)
+    zft[k, q] = summed(zt[1, q], art, r_a1t)
+    spread_out(zft, s_a2t, r_a2t)
     pl.semaphore_wait(tok.at[1], 2)
     for n in (-4, 4):
         pl.semaphore_signal(tok.at[2], inc=1, device_id=(z_off(n), f), device_id_type=MESH)
-    a2v += forward(zfv, s_a2v, r_a2v, s_fwv, r_fwv)
+    forward(zfv, r_a2v, s_fwv, r_fwv)
 
     def valid_features(c, at):
         lhs, rhs = [], []
@@ -344,15 +333,15 @@
                 ptl[at, p, 4, pl.ds(4 * h, 4), :] = cols[128 + 4 * p : 132 + 4 * p]
 
     valid_features(k, 1)
-    forwarded(zfv, s_fwv, r_fwv)
+    forwarded(zfv, r_fwv)
     valid_features(other, 0)
     tw_v = remote(pvl.at[0], pvtw, s_tw.at[1], r_tw.at[1], twin)
     tw_v.start()
     tw_v.wait_recv()
     pvl[1] = pvl[1] + pvtw[...]
-    b_v = to_chips(lambda to: pvl.at[1, to], lambda i: bvr.at[i], s_bv, r_bv)
-    a2t += forward(zft, s_a2t, r_a2t, s_fwt, r_fwt)
-    forwarded(zft, s_fwt, r_fwt)
+    to_chips(lambda to: pvl.at[1, to], lambda i: bvr.at[i], s_bv, r_bv)
+    forward(zft, r_a2t, s_fwt, r_fwt)
+    forwarded(zft, r_fwt)
     for i in range(5):
         train_pair(other, i)
     train_features(other, 0)
@@ -363,7 +352,7 @@
     train_features(k, 1)
     tw_t.wait_recv()
     ptl[1] = ptl[1] + pttw[...]
-    b_t = to_chips(lambda to: ptl.at[1, to], lambda i: btr.at[i], s_bt, r_bt)
+    to_chips(lambda to: ptl.at[1, to], lambda i: btr.at[i], s_bt, r_bt)
 
     par = lax.rem(zm, 2)
     slot = lax.div(zm, 2) * 2 + zr
@@ -371,11 +360,11 @@
     c_v = []
     for j in PAIR_OFFSETS:
         peer = (dp_at(y, 2 * lax.rem(zm + j, 8) + par), f)
-        c_v.append(remote(vs, vg.at[slot], s_c.at[j], r_c.at[slot], peer))
-    keep_v = pltpu.make_async_copy(vs, vg.at[slot], r_c.at[slot])
+        c_v.append(remote(vs, vg.at[slot], s_c, r_c, peer))
+    keep_v = pltpu.make_async_copy(vs, vg.at[slot], r_c)
 
     pl.semaphore_wait(tok.at[2], 2)
-    vs[...] = summed(pvl[1, q], b_v, bvr)
+    vs[...] = summed(pvl[1, q], bvr, r_bv)
     for cp in c_v[:7]:
         cp.start()
 
@@ -387,28 +376,23 @@
     def _():
         c_v[7].start()
 
-    total = summed(ptl[1, q], b_t, btr)
+    total = summed(ptl[1, q], btr, r_bt)
     ts[...] = total
     blk = 2 * y + zr
     tg[blk] = total
-    partners = (
-        (1 - y, zo, 2 * (1 - y) + 1 - zr),
-        (1 - y, z, 2 * (1 - y) + zr),
-        (y, zo, 2 * y + 1 - zr),
-    )
+    partners = ((1 - y, zo), (1 - y, z), (y, zo))
     q_t = [
-        remote(ts, tg.at[blk], s_q.at[j], r_q.at[j], (dp_at(py, pz), f))
-        for j, (py, pz, _) in enumerate(partners)
+        remote(ts, tg.at[blk], s_q, r_q, (dp_at(py, pz), f))
+        for py, pz in partners
     ]
     for cp in q_t:
         cp.start()
-    for i in range(8):
-        arrived(vs, vg.at[i], r_c.at[i])
+    arrived(vg, vg, r_c)
     vals = jnp.concatenate([vg[:, t].reshape(64, 128) for t in range(4)], axis=1)
     ones = jnp.ones((8, HALF), F32)
     nv = dot_nt(ones, vals * vals, lax.Precision.HIGHEST)
-    for j, (_, _, pb) in enumerate(partners):
-        remote(ts, tg.at[pb], s_q.at[j], r_q.at[j], twin).wait_recv()
+    three = tg.at[pl.ds(0, 3)]
+    arrived(three, three, r_q)
 
     tail = tg[:, 4].reshape(32, 128)
     row = iota((32, 128), 0) & 7
@@ -427,19 +411,16 @@
     msg_b = jnp.concatenate([cos[32:], half32(na), half32(nb)], axis=1)
     ds[:, 0] = msg_a.reshape(4, 8, 128)
     ds[:, 1] = msg_b.reshape(4, 8, 128)
-    d_c = []
     for by in range(2):
         for br in range(2):
             for i in range(4):
                 to_f = 8 * y + 2 * i + zr
                 b = 2 * by + br
-                j = 4 * b + i
                 here = jnp.logical_and(jnp.logical_and(y == by, zr == br), f == to_f)
                 cp = remote(
-                    ds.at[b], dr.at[f], s_d.at[j], r_d.at[f], (dp_at(by, 2 * zm + br), to_f)
+                    ds.at[b], dr.at[f], s_d, r_d, (dp_at(by, 2 * zm + br), to_f)
                 )
-                keep = pltpu.make_async_copy(ds.at[b], dr.at[f], r_d.at[f])
-                d_c.append((cp, here))
+                keep = pltpu.make_async_copy(ds.at[b], dr.at[f], r_d)
 
                 @pl.when(jnp.logical_not(here))
                 def _():
@@ -449,21 +430,26 @@
                 def _():
                     keep.start()
 
-    for cp in [tw_av, tw_at, tw_v, tw_t] + a1v + a1t + a2v + a2t + b_v + b_t + c_v[:7] + q_t:
+    for cp in (tw_av, tw_at, tw_v, tw_t):
         cp.wait_send()
-
-    @pl.when(jnp.logical_not(mine))
-    def _():
-        c_v[7].wait_send()
-
-    for cp, here in d_c:
-
-        @pl.when(jnp.logical_not(here))
+    for ref, sem in (
+        (arv, s_a1v), (art, s_a1t), (arv, s_a2v), (art, s_a2t), (zfv.at[0], s_fwv),
+        (zft.at[0], s_fwt), (bvr, s_bv), (btr, s_bt), (three, s_q),
+    ):
+        arrived(ref, ref, sem)
+    listed = jnp.logical_and(lax.div(f, 8) == y, lax.rem(f, 2) == zr)
+    for cond, full, sem in ((mine, vg, s_c), (listed, dr, s_d)):
+        most = full.at[pl.ds(0, full.shape[0] - 1)]
+
+        @pl.when(cond)
         def _():
-            cp.wait_send()
-
-    for i in range(16):
-        arrived(ds.at[0], dr.at[i], r_d.at[i])
+            arrived(most, most, sem)
+
+        @pl.when(jnp.logical_not(cond))
+        def _():
+            arrived(full, full, sem)
+
+    arrived(dr, dr, r_d)
     sa = dr[0, 0]
     sb = dr[0, 1]
     for i in range(1, 16):
@@ -521,17 +507,9 @@
         dma((8,)),
         dma((2, 3)),
         dma((4,)), dma((4,)),
-        dma((7,)), dma((7,)),
-        dma((7,)), dma((7,)),
-        dma((8,)), dma((8,)),
-        dma((7,)), dma((7,)),
-        dma((7,)), dma((7,)),
-        dma((8,)), dma((8,)),
-        dma((7,)), dma((7,)),
-        dma((7,)), dma((7,)),
-        dma((8,)), dma((8,)),
-        dma((3,)), dma((3,)),
-        dma((16,)), dma((16,)),
+        dma, dma, dma, dma((4,)), dma, dma,
+        dma, dma, dma, dma((4,)), dma, dma,
+        dma, dma, dma, dma, dma, dma, dma, dma, dma, dma,
         pltpu.SemaphoreType.REGULAR((3,)),
     ]
     return pl.pallas_call(

time: 49.7 us -> 48.4 us (0.974)
  Pallas kernels: 48.9 us -> 47.6 us
    pallas_call x1, Pallas kernels: 48.9 us -> 47.6 us  [body(): pl.pallas_call(kernel, name='features', out_shape=pltpu.VMEM((10, 16), F3...]
where the time goes in v5:
time: 48.4 us; the launch traced here: 48.2 us
  Pallas kernels  47.6 us (98%)
  local copies, waits for them, and re-layouts  0.6 us (1%)
    pallas_call x1, Pallas kernels, body(): pl.pallas_call(kernel, name='features', out_shape=pltpu.VMEM((10, 16), F3...  47.6 us

profile of v5, /device:TPU:1, one launch (start us, length us, event | category | flops | bytes accessed | tf_op | source)
XLA Modules:
  0.0 48.2 jit_solution(354728921527094538)
XLA Ops:
  0.0 47.6 %features.1 = f32[10,16]{1,0:T(8,128)S(1)} custom-call(bf16[960,512]{1,0:T(8,128)(2,1)} %bitcast.5, bf16[960,512]{1,0:T(8,128)(2,1)} %bitcast.6, s32[10,96]{1,0:T(8,128)} %lt.1, bf16[768,512]{1,0:T(8,128)(2,1)} %bitcast.7, bf16[768,512]{1,0:T(8,128)(2,1)} %bitcast.8, s32[8,96]{1,0:T(8,128)} %lv.1, bf16[64,512]{1,0:T(8,128)(2,1)} %ad.1, bf16[64,512]{1,0:T(8,128)(2,1)} %au.1, ...), custom_call_target="tpu_custom_call" | custom-call | tf_op jit(solution)/shard_map/features/pallas_call | solution.py:515
  47.6 0.6 %copy.14 = f32[10,16]{1,0:T(8,128)} copy(f32[10,16]{1,0:T(8,128)S(1)} %features.1) | data formatting | bytes 1280

commit v6 on v5

--- a/solution.py
+++ b/solution.py
@@ -298,7 +298,7 @@
             for a2_ in range(2):
                 pvl[at, :, 2 * a2_ + h] = part[:, a2_]
 
-    def train_pair(c, i):
+    def train_pair(c, i, at_dirs):
         t0 = (192 * i) // 128
         second = zft[c, :, t0 + 1] if t0 < 6 else zfv[c, :, 0]
         zg = jnp.concatenate([zft[c, :, t0].reshape(64, 128), second.reshape(64, 128)], axis=1)
@@ -316,11 +316,11 @@
                 num = m + (1.0 - BETA_FIRST) * g
                 second = v + (1.0 - BETA_SECOND) * g * g
                 den = second * lax.rsqrt(second) + ADAM_EPS
-                dirs[pl.ds(128 * i + 64 * s, 64), at] = (num / den).astype(BF16)
+                dirs[at_dirs, pl.ds(128 * i + 64 * s, 64), at] = (num / den).astype(BF16)
 
     def train_features(c, at):
-        l8 = dot(pm8[c], dirs[pl.ds(0, 512), :])
-        l2 = dot(pm2[c], dirs[pl.ds(512, 128), :])
+        l8 = dot(pm8[c], dirs[at, pl.ds(0, 512), :])
+        l2 = dot(pm2[c], dirs[at, pl.ds(512, 128), :])
         hi, lo = split(jnp.concatenate([l8, l2], axis=0))
         o = dot(jnp.concatenate([hi, lo], axis=0), fp[c])
         o = o[:160] + o[160:]
@@ -341,19 +341,15 @@
     pvl[1] = pvl[1] + pvtw[...]
     to_chips(lambda to: pvl.at[1, to], lambda i: bvr.at[i], s_bv, r_bv)
     forward(zft, r_a2t, s_fwt, r_fwt)
+    for i in range(5):
+        train_pair(k, i, 1)
     forwarded(zft, r_fwt)
     for i in range(5):
-        train_pair(other, i)
+        train_pair(other, i, 0)
     train_features(other, 0)
     tw_t = remote(ptl.at[0], pttw, s_tw.at[2], r_tw.at[2], twin)
     tw_t.start()
-    for i in range(5):
-        train_pair(k, i)
     train_features(k, 1)
-    tw_t.wait_recv()
-    ptl[1] = ptl[1] + pttw[...]
-    to_chips(lambda to: ptl.at[1, to], lambda i: btr.at[i], s_bt, r_bt)
-
     par = lax.rem(zm, 2)
     slot = lax.div(zm, 2) * 2 + zr
     mine = zr == par
@@ -375,6 +371,10 @@
     @pl.when(jnp.logical_not(mine))
     def _():
         c_v[7].start()
+
+    tw_t.wait_recv()
+    ptl[1] = ptl[1] + pttw[...]
+    to_chips(lambda to: ptl.at[1, to], lambda i: btr.at[i], s_bt, r_bt)
 
     total = summed(ptl[1, q], btr, r_bt)
     ts[...] = total
@@ -491,7 +491,7 @@
         pltpu.VMEM((8, 1024), F32),
         pltpu.VMEM((2, 128, HALF), BF16),
         pltpu.VMEM((2, 32, 128), BF16),
-        pltpu.VMEM((640, HALF), BF16),
+        pltpu.VMEM((2, 640, HALF), BF16),
         tile(2, 8, 4),
         tile(8, 4),
         tile(7, 4),

time: 48.4 us -> 48.4 us (level)
  no operation moved by 1% of the time
where the time goes in v6:
time: 48.4 us; the launch traced here: 48.2 us
  Pallas kernels  47.6 us (98%)
  local copies, waits for them, and re-layouts  0.6 us (1%)
    pallas_call x1, Pallas kernels, body(): pl.pallas_call(kernel, name='features', out_shape=pltpu.VMEM((10, 16), F3...  47.6 us

profile of v6, /device:TPU:1, one launch (start us, length us, event | category | flops | bytes accessed | tf_op | source)
XLA Modules:
  0.0 48.2 jit_solution(5145977354071532650)
XLA Ops:
  0.0 47.6 %features.1 = f32[10,16]{1,0:T(8,128)S(1)} custom-call(bf16[960,512]{1,0:T(8,128)(2,1)} %bitcast.5, bf16[960,512]{1,0:T(8,128)(2,1)} %bitcast.6, s32[10,96]{1,0:T(8,128)} %lt.1, bf16[768,512]{1,0:T(8,128)(2,1)} %bitcast.7, bf16[768,512]{1,0:T(8,128)(2,1)} %bitcast.8, s32[8,96]{1,0:T(8,128)} %lv.1, bf16[64,512]{1,0:T(8,128)(2,1)} %ad.1, bf16[64,512]{1,0:T(8,128)(2,1)} %au.1, ...), custom_call_target="tpu_custom_call" | custom-call | tf_op jit(solution)/shard_map/features/pallas_call | solution.py:515
  47.6 0.6 %copy.14 = f32[10,16]{1,0:T(8,128)} copy(f32[10,16]{1,0:T(8,128)S(1)} %features.1) | data formatting | bytes 1280

commit v7 on v6

--- a/solution.py
+++ b/solution.py
@@ -258,7 +258,11 @@
     pl.semaphore_wait(tok.at[1], 2)
     for n in (-4, 4):
         pl.semaphore_signal(tok.at[2], inc=1, device_id=(z_off(n), f), device_id_type=MESH)
-    forward(zfv, r_a2v, s_fwv, r_fwv)
+    for dx in (0, 1, 3, 2):
+        at = 2 * x + 1 - yh if dx == 0 else 2 * lax.rem(x + 4 - dx, 4)
+        come = zfv.at[k, pl.ds(at, 2 if dx else 1)]
+        arrived(come, come, r_a2v.at[dx])
+    remote(zfv.at[k], zfv.at[k], s_fwv, r_fwv, twin).start()
 
     def valid_features(c, at):
         lhs, rhs = [], []

time: 48.4 us -> 48.6 us (level)
  no operation moved by 1% of the time
where the time goes in v7:
time: 48.6 us; the launch traced here: 48.4 us
  Pallas kernels  47.8 us (98%)
  local copies, waits for them, and re-layouts  0.6 us (1%)
    pallas_call x1, Pallas kernels, body(): pl.pallas_call(kernel, name='features', out_shape=pltpu.VMEM((10, 16), F3...  47.8 us

profile of v7, /device:TPU:1, one launch (start us, length us, event | category | flops | bytes accessed | tf_op | source)
XLA Modules:
  0.0 48.4 jit_solution(4039243579311368533)
XLA Ops:
  0.0 47.8 %features.1 = f32[10,16]{1,0:T(8,128)S(1)} custom-call(bf16[960,512]{1,0:T(8,128)(2,1)} %bitcast.5, bf16[960,512]{1,0:T(8,128)(2,1)} %bitcast.6, s32[10,96]{1,0:T(8,128)} %lt.1, bf16[768,512]{1,0:T(8,128)(2,1)} %bitcast.7, bf16[768,512]{1,0:T(8,128)(2,1)} %bitcast.8, s32[8,96]{1,0:T(8,128)} %lv.1, bf16[64,512]{1,0:T(8,128)(2,1)} %ad.1, bf16[64,512]{1,0:T(8,128)(2,1)} %au.1, ...), custom_call_target="tpu_custom_call" | custom-call | tf_op jit(solution)/shard_map/features/pallas_call | solution.py:519
  47.8 0.6 %copy.14 = f32[10,16]{1,0:T(8,128)} copy(f32[10,16]{1,0:T(8,128)S(1)} %features.1) | data formatting | bytes 1280
